TPU v7x, 128 devices: a whole 4x4x4 slice. The times are simulated.
128 devices in a mesh: dp: 8 (over x, core), seq: 16 (over y, z).
Axes of the slice: x: 4, y: 4, z: 4, core: 2. Of those that a mesh axis runs over, the one named last changes fastest.
Arguments:
- inputs: float32 [16, 1024, 512], P('dp', 'seq'), may hold values from -6 to 6
- cotangent: float32 [16, 1024, 512], P('dp', 'seq'), may hold values from -6 to 6
- lengths: int32 [16], P('dp'), may hold values from 1 to 1024, as said below
- gain_first: bfloat16 [512], P(('dp', 'seq')), may hold values from 0.099609375 to 1.8984375
- proj_in: bfloat16 [512, 1024], P(('dp', 'seq')), may hold values from -0.25 to 0.25
- sub_kernels: bfloat16 [5, 32, 512], P(None, None, ('dp', 'seq')), may hold values from -6 to 6
- skip_gain: bfloat16 [512], P(('dp', 'seq')), may hold values from -3 to 3
- proj_out: bfloat16 [512, 512], P(('dp', 'seq')), may hold values from -0.5 to 0.5
- gain_second: bfloat16 [512], P(('dp', 'seq')), may hold values from 0.099609375 to 1.8984375
- mlp_up: bfloat16 [512, 2048], P(('dp', 'seq')), may hold values from -0.25 to 0.25
- mlp_down: bfloat16 [2048, 512], P(('dp', 'seq')), may hold values from -0.1875 to 0.1875
Outputs:
- outputs: float32 [16, 1024, 512], P('dp', 'seq')
- grad_inputs: float32 [16, 1024, 512], P('dp', 'seq')
- grad_gain_first: float32 [512], P(('dp', 'seq'))
- grad_proj_in: float32 [512, 1024], P(('dp', 'seq'))
- grad_sub_kernels: float32 [5, 32, 512], P(None, None, ('dp', 'seq'))
- grad_skip_gain: float32 [512], P(('dp', 'seq'))
- grad_proj_out: float32 [512, 512], P(('dp', 'seq'))
- grad_gain_second: float32 [512], P(('dp', 'seq'))
- grad_mlp_up: float32 [512, 2048], P(('dp', 'seq'))
- grad_mlp_down: float32 [2048, 512], P(('dp', 'seq'))
Inputs may be any that keep to these rules, and one draw needn't show every extreme that they name: `lengths`: each aligned group of 2 sequences (those of one index of dp) holds one sequence of length 1024; positions at or past a sequence's length are padding.
All inputs are finite; a program needn't handle non-finite values.
Results may differ from a plain program's by a relative error of at most 0.013.
Values may be sent and summed in bfloat16 or wider, within the bound.
A program may use at most 128 MiB of HBM per device.

v0:
```python
from functools import partial

import jax
import jax.numpy as jnp
from jax import lax
from jax.sharding import PartitionSpec as P

EPSILON = 1e-05


def shifted(shard, axis, by):
    count = lax.axis_size(axis)
    pairs = [(i, i + by) for i in range(count) if 0 <= i + by < count]
    return lax.ppermute(shard, axis, pairs)


def layer_norm(values, gain_vec):
    centered = values - jnp.mean(values, axis=-1, keepdims=True)
    variance = jnp.mean(centered * centered, axis=-1, keepdims=True)
    return centered * lax.rsqrt(variance + EPSILON) * gain_vec


def build_kernel(sub_taps, length):
    pieces = []
    for octave in range(sub_taps.shape[0]):
        pieces.append(jnp.repeat(sub_taps[octave], 2**octave, axis=0) * 0.5**octave)
    kernel = jnp.concatenate(pieces, axis=0)
    kernel = kernel * lax.rsqrt(jnp.sum(kernel * kernel, axis=0, keepdims=True) + EPSILON)
    if kernel.shape[0] >= length:
        return kernel[:length]
    return jnp.pad(kernel, ((0, length - kernel.shape[0]), (0, 0)))


def exact_gelu(values):
    return jax.nn.gelu(values, approximate=False)


def toeplitz_block(kernel_pad, offset, block_rows):
    first_tap = offset + kernel_pad.shape[0] // 2 - block_rows + 1
    window = lax.dynamic_slice_in_dim(kernel_pad, first_tap, 2 * block_rows - 1, 0)
    tap_index = jnp.arange(block_rows)[:, None] - jnp.arange(block_rows)[None, :] + block_rows - 1
    return jnp.take(window, tap_index, axis=0)


def apply_block(kernel_pad, offset, source):
    toeplitz = toeplitz_block(kernel_pad, offset, source.shape[1])
    return jnp.einsum("abc,sbc->sac", toeplitz, source, preferred_element_type=jnp.float32)


def block_grads(kernel_pad, offset, grad_out, reversed_in):
    block_rows = grad_out.shape[1]
    toeplitz = toeplitz_block(kernel_pad, offset, block_rows)
    grad_in = jnp.einsum("abc,sac->sbc", toeplitz, grad_out, preferred_element_type=jnp.float32)
    product = jnp.einsum("sac,sbc->abc", grad_out, reversed_in, preferred_element_type=jnp.float32)
    skewed = product.reshape(block_rows + 1, block_rows, product.shape[2])
    row_iota = jnp.arange(block_rows + 1)[:, None, None]
    col_iota = jnp.arange(block_rows)[None, :, None]
    lower = jnp.sum(jnp.where(row_iota <= col_iota, skewed, 0.0), axis=0)
    upper = jnp.sum(jnp.where(row_iota > col_iota, skewed, 0.0), axis=0)[: block_rows - 1]
    return (grad_in, jnp.concatenate([lower, upper], axis=0))


def add_taps(tap_grads, offset, taps, block_rows):
    first_tap = offset + tap_grads.shape[0] // 2 - block_rows + 1
    current = lax.dynamic_slice_in_dim(tap_grads, first_tap, taps.shape[0], 0)
    return lax.dynamic_update_slice_in_dim(tap_grads, current + taps, first_tap, 0)


def body(
    inputs,
    cotangent,
    lengths,
    gain_first,
    proj_in,
    sub_kernels,
    skip_gain,
    proj_out,
    gain_second,
    mlp_up,
    mlp_down,
):
    seq_count, block_rows, width = inputs.shape
    devices_seq = lax.axis_size("seq")
    slot_rows = devices_seq * block_rows
    my_start = lax.axis_index("seq") * block_rows
    positions = my_start + jnp.arange(block_rows, dtype=jnp.int32)
    row_mask = (positions[None, :] < lengths[:, None]).astype(jnp.float32)[:, :, None]
    gain_one, w_in_all, sub_all, skip_all, w_out_all, gain_two, up_all, down_all = (
        lax.all_gather(gain_first, ("dp", "seq"), axis=0, tiled=True),
        lax.all_gather(proj_in, ("dp", "seq"), axis=0, tiled=True),
        lax.all_gather(sub_kernels, ("dp", "seq"), axis=2, tiled=True),
        lax.all_gather(skip_gain, ("dp", "seq"), axis=0, tiled=True),
        lax.all_gather(proj_out, ("dp", "seq"), axis=0, tiled=True),
        lax.all_gather(gain_second, ("dp", "seq"), axis=0, tiled=True),
        lax.all_gather(mlp_up, ("dp", "seq"), axis=0, tiled=True),
        lax.all_gather(mlp_down, ("dp", "seq"), axis=0, tiled=True),
    )
    normed, norm_pull = jax.vjp(layer_norm, inputs, gain_one.astype(jnp.float32))
    normed_low = normed.astype(jnp.bfloat16)
    projected = jnp.einsum("sbd,de->sbe", normed_low, w_in_all, preferred_element_type=jnp.float32)
    values = projected[..., :width]
    gates = projected[..., width:]
    kernel, kernel_pull = jax.vjp(
        partial(build_kernel, length=slot_rows), sub_all.astype(jnp.float32)
    )
    kernel_pad = jnp.concatenate(
        [jnp.zeros((slot_rows, width), jnp.bfloat16), kernel.astype(jnp.bfloat16)], axis=0
    )
    values_low = values.astype(jnp.bfloat16)

    def forward_turn(turn, state):
        moving, total = state
        moving = shifted(moving, "seq", 1)
        return (moving, total + apply_block(kernel_pad, turn * block_rows, moving))

    moved_last, conv = lax.fori_loop(
        1, devices_seq, forward_turn, (values_low, apply_block(kernel_pad, 0, values_low))
    )
    skip_vec = skip_all.astype(jnp.float32)
    mixed = conv + skip_vec * values
    gated, gate_pull = jax.vjp(exact_gelu, gates)
    branch_in = (mixed * gated).astype(jnp.bfloat16)
    branch_out = jnp.einsum("sbd,de->sbe", branch_in, w_out_all, preferred_element_type=jnp.float32)
    hidden = inputs + row_mask * branch_out
    normed_two, norm_two_pull = jax.vjp(layer_norm, hidden, gain_two.astype(jnp.float32))
    normed_two_low = normed_two.astype(jnp.bfloat16)
    up_proj = jnp.einsum("sbd,df->sbf", normed_two_low, up_all, preferred_element_type=jnp.float32)
    activated, act_pull = jax.vjp(exact_gelu, up_proj)
    activated_low = activated.astype(jnp.bfloat16)
    mlp_out = jnp.einsum("sbf,fd->sbd", activated_low, down_all, preferred_element_type=jnp.float32)
    outputs = hidden + row_mask * mlp_out
    grad_mlp_out = (row_mask * cotangent).astype(jnp.bfloat16)
    grad_down = jnp.einsum(
        "sbf,sbd->fd", activated_low, grad_mlp_out, preferred_element_type=jnp.float32
    )
    grad_act = jnp.einsum("sbd,fd->sbf", grad_mlp_out, down_all, preferred_element_type=jnp.float32)
    grad_up_proj = act_pull(grad_act)[0].astype(jnp.bfloat16)
    grad_up = jnp.einsum(
        "sbd,sbf->df", normed_two_low, grad_up_proj, preferred_element_type=jnp.float32
    )
    grad_normed_two = jnp.einsum(
        "sbf,df->sbd", grad_up_proj, up_all, preferred_element_type=jnp.float32
    )
    grad_hidden_norm, grad_gain_two = norm_two_pull(grad_normed_two)
    grad_hidden = cotangent + grad_hidden_norm
    grad_branch = (row_mask * grad_hidden).astype(jnp.bfloat16)
    grad_w_out = jnp.einsum(
        "sbd,sbe->de", branch_in, grad_branch, preferred_element_type=jnp.float32
    )
    grad_branch_in = jnp.einsum(
        "sbe,de->sbd", grad_branch, w_out_all, preferred_element_type=jnp.float32
    )
    grad_mixed = grad_branch_in * gated
    grad_gates = gate_pull(grad_branch_in * mixed)[0]
    grad_skip = jnp.sum(grad_mixed * values, axis=(0, 1))
    grad_conv = grad_mixed.astype(jnp.bfloat16)
    empty_taps = jnp.zeros((2 * slot_rows, width), jnp.float32)
    reversed_in = jnp.pad(values_low[:, ::-1], ((0, 0), (0, 1), (0, 0)))
    grad_first, taps_first = block_grads(kernel_pad, 0, grad_conv, reversed_in)

    def backward_turn(turn, state):
        moving, grad_total, tap_total = state
        moving = shifted(moving, "seq", -1)
        offset = turn * block_rows
        term, taps = block_grads(kernel_pad, offset, moving, reversed_in)
        return (moving, grad_total + term, add_taps(tap_total, offset, taps, block_rows))

    moved_last, grad_values_conv, tap_grads = lax.fori_loop(
        1,
        devices_seq,
        backward_turn,
        (grad_conv, grad_first, add_taps(empty_taps, 0, taps_first, block_rows)),
    )
    grad_sub = kernel_pull(tap_grads[slot_rows:])[0]
    grad_projected = jnp.concatenate(
        [grad_values_conv + skip_vec * grad_mixed, grad_gates], axis=-1
    ).astype(jnp.bfloat16)
    grad_w_in = jnp.einsum(
        "sbd,sbe->de", normed_low, grad_projected, preferred_element_type=jnp.float32
    )
    grad_normed = jnp.einsum(
        "sbe,de->sbd", grad_projected, w_in_all, preferred_element_type=jnp.float32
    )
    grad_input_norm, grad_gain_one = norm_pull(grad_normed)
    grad_inputs = grad_hidden + grad_input_norm
    (
        shard_gain_one,
        shard_w_in,
        shard_sub,
        shard_skip,
        shard_w_out,
        shard_gain_two,
        shard_up,
        shard_down,
    ) = (
        lax.psum_scatter(grad_gain_one, ("dp", "seq"), scatter_dimension=0, tiled=True),
        lax.psum_scatter(grad_w_in, ("dp", "seq"), scatter_dimension=0, tiled=True),
        lax.psum_scatter(grad_sub, ("dp", "seq"), scatter_dimension=2, tiled=True),
        lax.psum_scatter(grad_skip, ("dp", "seq"), scatter_dimension=0, tiled=True),
        lax.psum_scatter(grad_w_out, ("dp", "seq"), scatter_dimension=0, tiled=True),
        lax.psum_scatter(grad_gain_two, ("dp", "seq"), scatter_dimension=0, tiled=True),
        lax.psum_scatter(grad_up, ("dp", "seq"), scatter_dimension=0, tiled=True),
        lax.psum_scatter(grad_down, ("dp", "seq"), scatter_dimension=0, tiled=True),
    )
    return (
        outputs,
        grad_inputs,
        shard_gain_one,
        shard_w_in,
        shard_sub,
        shard_skip,
        shard_w_out,
        shard_gain_two,
        shard_up,
        shard_down,
    )


def solution(mesh):
    in_specs = (
        P("dp", "seq", None),
        P("dp", "seq", None),
        P("dp"),
        P(("dp", "seq")),
        P(("dp", "seq"), None),
        P(None, None, ("dp", "seq")),
        P(("dp", "seq")),
        P(("dp", "seq"), None),
        P(("dp", "seq")),
        P(("dp", "seq"), None),
        P(("dp", "seq"), None),
    )
    out_specs = (
        P("dp", "seq", None),
        P("dp", "seq", None),
        P(("dp", "seq")),
        P(("dp", "seq"), None),
        P(None, None, ("dp", "seq")),
        P(("dp", "seq")),
        P(("dp", "seq"), None),
        P(("dp", "seq")),
        P(("dp", "seq"), None),
        P(("dp", "seq"), None),
    )
    return jax.shard_map(body, mesh=mesh, in_specs=in_specs, out_specs=out_specs, check_vma=False)
```

profile of v0, /device:TPU:0, one launch (start us, length us, event | category | flops | bytes accessed | tf_op | source)
XLA Modules:
  0.0 3651.9 jit_solution(5966979422760035751)
XLA Ops:
  10.1 61.6 %all_gather.26 = bf16[5,32,512]{1,0,2:T(8,128)(2,1)S(1)} all-gather(bf16[5,32,4]{1,0,2:T(8,128)(2,1)S(1)} %copy.54), channel_id=1, replica_groups=mesh['dp'=8,'seq'=16] {'dp','seq'}, dimensions={2}, use_global_device_ids=true | all-gather | bytes 165120 | tf_op jit(solution)/shard_map/all_gather | solution.py:91
  75.0 65.4 %all-reduce.21 = (bf16[512]{0:T(512)(128)(2,1)S(1)}, bf16[512]{0:T(512)(128)(2,1)S(1)}, bf16[512]{0:T(512)(128)(2,1)S(1)}) all-reduce(bf16[512]{0:T(512)(128)(2,1)S(1)} %dynamic-update-slice, bf16[512]{0:T(512)(128)(2,1)S(1)} %dynamic-update-slice.1, bf16[512]{0:T(512)(128)(2,1)S(1)} %dynamic-update-slice.2), channel_id=1, replica_groups=mesh['dp'=8,'seq'=16] {'dp','seq'}, use_global_device_ids=true, to_apply=%add.10 | all-reduce | flops 1536 | bytes 6144
  145.3 17.3 gather_fusion.2
  177.2 51.0 %all-gather.1 = bf16[128,4,512]{2,1,0:T(4,128)(2,1)S(1)} all-gather(bf16[1,4,512]{2,1,0:T(4,128)(2,1)S(1)} %bitcast.123), channel_id=1, replica_groups=mesh['dp'=8,'seq'=16] {'dp','seq'}, dimensions={0}, use_global_device_ids=true | all-gather | bytes 528384 | tf_op jit(solution)/shard_map/all_gather | solution.py:93
  238.6 643.3 %while.40 = (s32[]{:T(128)}, bf16[2,64,512]{1,0,2:T(2,128)(2,1)S(1)}, f32[2,64,512]{1,0,2:T(2,128)S(1)}, bf16[2048,512]{1,0:T(8,128)(2,1)}, s32[]{:T(128)}, /*index=5*/s32[]{:T(128)}, s32[]{:T(128)}, s32[]{:T(128)}, s32[]{:T(128)}) while((s32[]{:T(128)}, bf16[2,64,512]{1,0,2:T(2,128)(2,1)S(1)}, f32[2,64,512]{1,0,2:T(2,128)S(1)}, ...), condition=%wide.region_4.6_spmd, body=%wide.region_3.5_spmd.sunk | while | flops 10608647 | bytes 22780100 | solution.py:116
  241.9 17.3 gather_fusion
  284.2 17.3 gather_fusion
  327.9 17.3 gather_fusion
  370.9 17.3 gather_fusion
  412.6 17.3 gather_fusion
  455.6 17.3 gather_fusion
  499.0 17.3 gather_fusion
  542.7 17.3 gather_fusion
  584.7 17.3 gather_fusion
  626.7 17.3 gather_fusion
  670.7 17.3 gather_fusion
  715.1 17.3 gather_fusion
  756.8 17.3 gather_fusion
  799.8 17.3 gather_fusion
  843.2 17.3 gather_fusion
  966.0 1200.3 %while.41 = (s32[]{:T(128)}, bf16[2,64,512]{1,0,2:T(2,128)(2,1)S(1)}, f32[2,64,512]{1,0,2:T(2,128)}, f32[2048,512]{1,0:T(8,128)}, bf16[2048,512]{1,0:T(8,128)(2,...) while((s32[]{:T(128)}, ...), condition=%wide.region_14.16_spmd, body=%wide.region_11.0_spmd.sunk | while | flops 27720840 | bytes 75741648 | solution.py:168
  968.5 17.3 gather_fusion.1
  1048.6 17.3 gather_fusion.1
  1208.6 17.3 gather_fusion.1
  1288.6 17.3 gather_fusion.1
  1368.7 17.3 gather_fusion.1
  1448.7 17.3 gather_fusion.1
  1528.7 17.3 gather_fusion.1
  2184.6 91.2 %all-reduce.19 = (f32[512]{0:T(512)S(1)}, f32[512]{0:T(512)S(1)}, f32[512]{0:T(512)S(1)}) all-reduce(f32[512]{0:T(512)S(1)} %get-tuple-element.427, f32[512]{0:T(512)S(1)} %copy-done.54, f32[512]{0:T(512)S(1)} %copy-done.52), channel_id=2, replica_groups=mesh['dp'=8,'seq'=16] {'dp','seq'}, use_global_device_ids=true, to_apply=%region_18.20.clone | all-reduce | flops 1536 | bytes 12288
  2281.1 556.3 %reduce-scatter.3.cloned.1.call-done = f32[5,32,4]{1,0,2:T(8,128)} async-done(((f32[5,32,512]{1,0,2:T(8,128)}), f32[5,32,4]{1,0,2:T(8,128)}) %reduce-scatter.3.cloned.1.call-update) | async-done | bytes 2576 | tf_op jit(solution)/shard_map/reduce_scatter | solution.py:198
  2838.7 160.2 %all-reduce.24.cloned.1.call-done = (f32[512,1024]{1,0:T(8,128)}, f32[512,512]{1,0:T(8,128)}, f32[512,2048]{1,0:T(8,128)}) async-done(((f32[512,1024]{1,0:T(8,128)}, f32[512,512]{1,0:T(8,128)}, f32[512,2048]{1,0:T(8,128)}), (f32[512,1024]{1,0:T(8,128)}, f32[512,512]{1,0:T(8,128)}, f32[512,2048]{1,0:T(8,128)})) %all-reduce.24.cloned.1.call-update) | async-done | bytes 7340048
  3003.1 641.8 %reduce-scatter.5.cloned.1.call-done = f32[16,512]{1,0:T(8,128)} async-done(((f32[2048,512]{1,0:T(8,128)}), f32[16,512]{1,0:T(8,128)}) %reduce-scatter.5.cloned.1.call-update) | async-done | bytes 32784 | tf_op jit(solution)/shard_map/reduce_scatter | solution.py:203
  (646 shorter events, 1609.0 us)
Async XLA Ops:
  7.2 221.3 %all-gather.9.cloned.1.call-start = ((), (), s32[]{:S(2)}) async-start(), calls=%async_computation.5 | async-start | bytes 1056768 | tf_op jit(solution)/shard_map/all_gather | solution.py:90
  7.9 878.4 %all-gather.11.cloned.1.call-start = ((), (), s32[]{:S(2)}) async-start(), calls=%async_computation.6 | async-start | bytes 2113536 | tf_op jit(solution)/shard_map/all_gather | solution.py:95
  8.7 901.8 %all-gather.7.cloned.1.call-start = ((), (), s32[]{:S(2)}) async-start(), calls=%async_computation.2 | async-start | bytes 2113536 | tf_op jit(solution)/shard_map/all_gather | solution.py:96
  9.4 2828.0 %reduce-scatter.3.cloned.1.call-start = ((), (), s32[]{:S(2)}) async-start(), calls=%async_computation.3 | async-start | bytes 2113536 | tf_op jit(solution)/shard_map/reduce_scatter | solution.py:198
  238.6 33.6 collective-permute-start
  280.6 33.9 collective-permute-start
  322.9 35.2 collective-permute-start
  366.6 34.6 collective-permute-start
  409.6 33.4 collective-permute-start
  451.3 34.6 collective-permute-start
  494.3 35.0 collective-permute-start
  537.7 35.4 collective-permute-start
  581.4 33.6 collective-permute-start
  623.4 33.6 collective-permute-start
  665.4 35.6 collective-permute-start
  709.4 36.0 collective-permute-start
  753.8 33.3 collective-permute-start
  795.5 34.7 collective-permute-start
  838.5 35.0 collective-permute-start
  966.0 32.8 collective-permute-start.1
  1046.2 32.7 collective-permute-start.1
  1126.2 32.7 collective-permute-start.1
  1206.3 32.7 collective-permute-start.1
  1286.3 32.7 collective-permute-start.1
  1366.3 32.7 collective-permute-start.1
  1446.3 32.7 collective-permute-start.1
  1526.3 32.7 collective-permute-start.1
  1606.3 32.7 collective-permute-start.1
  1686.4 32.7 collective-permute-start.1
  2006.4 32.7 collective-permute-start.1
  2173.7 825.3 %all-reduce.24.cloned.1.call-start = ((), (), s32[]{:S(2)}) async-start(), calls=%async_computation.7 | async-start | bytes 14680064
  2179.8 1465.0 %reduce-scatter.5.cloned.1.call-start = ((), (), s32[]{:S(2)}) async-start(), calls=%async_computation.4 | async-start | bytes 4227072 | tf_op jit(solution)/shard_map/reduce_scatter | solution.py:203
  (60 other events, 6718.4 us)
Sparse Core Ops, SparseCore 0:
  10.8 66.0 all-gather.8
  79.8 63.0 all-gather.10
  145.9 62.7 all-gather.6
  2173.8 663.5 reduce-scatter.2
  2843.8 155.1 all-reduce.23
  3001.9 642.9 reduce-scatter.4
where the time goes:
time: 3670 us; the launch traced here: 3650 us
  local copies, waits for them, and re-layouts  1430 us (39%)
  waiting for transfers between devices  1360 us (37%)
  matrix products  371 us (10%)
  blocking collectives  269 us (7%)
  other arithmetic  135 us (4%)
  starting transfers between devices  66.5 us (2%)
    gather x62, local copies, waits for them, and re-layouts, toeplitz_block(): return jnp.take(window, tap_index, axis=0)  939 us
    reduce_scatter x1, waiting for transfers between devices, body(): lax.psum_scatter(grad_down, ('dp', 'seq'), scatter_dimension=0, tiled=True)  642 us
    reduce_scatter x1, waiting for transfers between devices, body(): lax.psum_scatter(grad_sub, ('dp', 'seq'), scatter_dimension=2, tiled=True)  556 us
    transpose x16, local copies, waits for them, and re-layouts, block_grads(): jnp.einsum('sac,sbc->abc', grad_out, reversed_in, preferred_element_type=...  248 us
    unnamed x7, waiting for transfers between devices  162 us
    unnamed x2, blocking collectives  157 us
    reshape x16, local copies, waits for them, and re-layouts, block_grads(): skewed = product.reshape(block_rows + 1, block_rows, product.shape[2])  154 us
    dot_general x16, matrix products, apply_block(): jnp.einsum('abc,sbc->sac', toeplitz, source, preferred_element_type=jnp.f...  131 us
  transfers between devices with their start and end apart: 36, of which 3 were waited for; matrix products, arithmetic and copies ran while one was open for 32% of the time, Pallas kernels for 0%

commit v1 on v0

v1 whole, which is shorter than its diff:
```python
import math

import jax
import jax.numpy as jnp
import ml_dtypes
import numpy as np
from jax import lax
from jax.experimental import pallas as pl
from jax.experimental.pallas import tpu as pltpu
from jax.sharding import PartitionSpec as P

EPSILON = 1e-05
D = 512
FF = 2048
SLOT = 1024
NSUB = 5
SUBTAPS = 32
TAPS = NSUB * SUBTAPS
F32 = jnp.float32
BF16 = jnp.bfloat16
MESH = pl.DeviceIdType.MESH

VAL, EXT, UPA, GAT, OUT, UPB, END, WIDE = 0, 512, 768, 1792, 2304, 2816, 3840, 4096
XE, XU, YG, YU = (VAL, UPA), (UPA, GAT), (GAT, UPB), (UPB, END)


def transforms():
    place = np.arange(SLOT)
    angle = 2 * np.pi * ((2 * place[:, None] + 1) * place[None, :] % (4 * SLOT)) / (4 * SLOT)
    forward = np.concatenate([np.cos(angle), -np.sin(angle)], axis=0)
    inverse = forward.T / SLOT
    repeat = np.zeros((SLOT, 256))
    first = 0
    for octave in range(NSUB):
        for tap in range(SUBTAPS):
            repeat[first : first + 2**octave, octave * SUBTAPS + tap] = 0.5**octave
            first += 2**octave
    half = np.stack([inverse[:512], inverse[512:]])
    return tuple(a.astype(ml_dtypes.bfloat16) for a in (forward, half, forward @ repeat))


def nn(a, b):
    return lax.dot_general(a, b, (((1,), (0,)), ((), ())), preferred_element_type=F32)


def nt(a, b):
    return lax.dot_general(a, b, (((1,), (1,)), ((), ())), preferred_element_type=F32)


def tn(a, b):
    return lax.dot_general(a, b, (((0,), (0,)), ((), ())), preferred_element_type=F32)


def gelu_parts(v):
    cdf = 0.5 * (1.0 + lax.erf(v * math.sqrt(0.5)))
    slope = cdf + v * (jnp.exp(-0.5 * v * v) * (1.0 / math.sqrt(2 * math.pi)))
    return v * cdf, slope


def swap_matrix():
    row = lax.broadcasted_iota(jnp.int32, (64, 64), 0)
    col = lax.broadcasted_iota(jnp.int32, (64, 64), 1)
    source = ((row >> 2) & 3) * 16 + (row >> 4) * 4 + (row & 3)
    return jnp.where(col == source, 1.0, 0.0).astype(BF16)


def fused(
    x_ref, cot_ref, len_ref, pack_ref, down_ref, dft_hbm, inv_hbm, rep_hbm,
    out_ref, gin_ref, gpack_ref, gdown_ref,
    zin, wb, wd, dft, inv, rep,
    xh1, inv1, nlow, val, gated, dgel, mixed, bi, hid, xh2, n2l, gmo, gact, act, gup, ghid, gb, ggate, prods,
    vsend, vin, ysend, cin, gsend, gvin, csend, gcin, spec_v, spec_k, spec_g, spec_y,
    acc, csw, crw, s2, r2, acc2, s3, r3, tail,
    accd, csd, crd, s2d, r2d, acc2d, s3d, r3d, acc3d, s4d, r4d, s4, r4,
    send_sem, recv_sem, local_sem,
):
    dp, j = lax.axis_index("dp"), lax.axis_index("seq")
    x, c = dp // 2, dp % 2
    y, z = j // 4, j % 4
    half, pair = j % 2, j // 2
    group = pair % 4

    def turn(v, by):
        return lax.rem(v + by, 4)

    def x_at(v):
        return (v * 2 + c, j)

    def y_at(v):
        return (dp, v * 4 + z)

    def z_at(v):
        return (dp, y * 4 + v)

    sibling = (x * 2 + 1 - c, j)

    barrier = pltpu.get_barrier_semaphore()
    partners = [sibling] + [x_at(turn(x, i)) for i in (1, 2, 3)]
    partners += [(dp, lax.rem(j + i, 16)) for i in range(1, 16)]
    for partner in partners:
        pl.semaphore_signal(barrier, inc=1, device_id=partner, device_id_type=MESH)

    loads = [
        pltpu.make_async_copy(rep_hbm, rep, local_sem.at[0]),
        pltpu.make_async_copy(dft_hbm, dft, local_sem.at[1]),
        pltpu.make_async_copy(inv_hbm.at[half], inv, local_sem.at[2]),
    ]
    for load in loads:
        load.start()

    zin[z] = pack_ref[...]
    wd[x, c, y, z] = down_ref[...]

    pl.semaphore_wait(barrier, len(partners))

    started = []

    def push(src, dst, device):
        at = len(started)
        copy = pltpu.make_async_remote_copy(
            src_ref=src,
            dst_ref=dst,
            send_sem=send_sem.at[at],
            recv_sem=recv_sem.at[at],
            device_id=device,
            device_id_type=MESH,
        )
        copy.start()
        started.append(copy)
        return copy

    def ring(me, at, src, dst):
        return [push(src(turn(me, i)), dst(i), at(turn(me, i))) for i in (1, 2, 3)]

    def arrived(copies):
        for copy in copies:
            copy.wait_recv()

    def same(me, at, ref):
        return ring(me, at, lambda to: ref, lambda i: ref)

    got_z = same(z, z_at, zin.at[z])
    got_dx = same(x, x_at, wd.at[x, c, y, z])

    source = x_ref[...]
    centered = source - jnp.mean(source, axis=1, keepdims=True)
    inv_one = lax.rsqrt(jnp.mean(centered * centered, axis=1, keepdims=True) + EPSILON)
    inv1[...] = inv_one
    xh1[...] = centered * inv_one

    row = lax.broadcasted_iota(jnp.int32, (128, 1), 0)
    limit = jnp.where(row < 64, len_ref[0], len_ref[1])
    mask = jnp.where((row & 63) + j * 64 < limit, 1.0, 0.0)

    swap = swap_matrix()
    arrived(got_z)
    rows = nn(swap, zin[...].reshape(64, 1024)).astype(BF16)
    for u in range(4):
        wb[x, c, y, :, 1024 * u : 1024 * (u + 1)] = rows[16 * u : 16 * u + 16]

    def cols(ends):
        return pl.ds(ends[0], ends[1] - ends[0])

    def first_x(p):
        return same(y, y_at, wb.at[x, c, y, :, cols(p)])

    def first_y(p):
        return same(x, x_at, wb.at[x, c, y, :, cols(p)])

    def bulk_x(p):
        return same(x, x_at, wb.at[x, c, :, :, cols(p)])

    def bulk_y(p):
        return same(y, y_at, wb.at[:, c, y, :, cols(p)])

    def to_sibling(p):
        ref = wb.at[:, c, :, :, cols(p)]
        return [push(ref, ref, sibling)]

    got_xe, got_yg, got_xu, got_yu = first_x(XE), first_y(YG), first_x(XU), first_y(YU)
    arrived(got_dx)
    got_dy = same(y, y_at, wd.at[:, c, y, z])
    arrived(got_xe)
    got_xe = bulk_x(XE)
    arrived(got_yg)
    got_yg = bulk_y(YG)
    arrived(got_dy)
    got_dz = same(z, z_at, wd.at[:, c, :, z])
    arrived(got_xu)
    arrived(got_yu)
    arrived(got_xe)
    got_xe = to_sibling(XE)
    arrived(got_yg)
    got_yg = to_sibling(YG)
    got_xu = bulk_x(XU)
    got_yu = bulk_y(YU)

    def weight(first, width):
        return wb[:, :, :, :, first : first + width].reshape(512, width)

    arrived(got_xe)
    pick = jnp.where(
        lax.broadcasted_iota(jnp.int32, (8, 128), 1)
        == lax.broadcasted_iota(jnp.int32, (8, 128), 0) + (TAPS - 128),
        1.0,
        0.0,
    ).astype(BF16)
    gains = nt(pick, weight(EXT + 128, 128))
    gain_one, gain_two, skip = gains[0:1], gains[1:2], gains[2:3]
    nlow[...] = (xh1[...] * gain_one).astype(BF16)
    values = nn(nlow[...], weight(VAL, 512))
    val[...] = values
    low = values.astype(BF16)
    for b in range(2):
        for g in range(4):
            vsend[4 * b + g] = low[64 * b : 64 * b + 64, 128 * g : 128 * g + 128]

    def scatter(src, dst):
        copies = []
        for i in range(1, 16):
            to = lax.rem(j + i, 16)
            copies.append(push(src.at[to // 2], dst.at[j], (dp, to)))
        dst[j] = src[pair]
        return copies

    def give_back(src, dst):
        base = len(started)
        copies = []
        for i in range(8):
            to = 8 * half + i
            copy = pltpu.make_async_remote_copy(
                src_ref=src.at[i],
                dst_ref=dst.at[pair],
                send_sem=send_sem.at[base + i],
                recv_sem=recv_sem.at[base + pair],
                device_id=(dp, to),
                device_id_type=MESH,
            )

            @pl.when(to != j)
            def _(copy=copy):
                copy.start()

            @pl.when(to == j)
            def _(i=i):
                dst[pair] = src[i]

            copies.append((copy, to))
            started.append(None)
        receipts = []
        for q in range(8):
            receipt = pltpu.make_async_remote_copy(
                src_ref=src.at[q],
                dst_ref=dst.at[q],
                send_sem=send_sem.at[base + q],
                recv_sem=recv_sem.at[base + q],
                device_id=sibling,
                device_id_type=MESH,
            )
            receipts.append((receipt, 2 * q + j // 8))
        return copies, receipts

    def taken_back(receipts):
        for receipt, sender in receipts:

            @pl.when(sender != j)
            def _(receipt=receipt):
                receipt.wait_recv()

    def sent_back(copies):
        for copy, to in copies:

            @pl.when(to != j)
            def _(copy=copy):
                copy.wait_send()

    got_v = scatter(vsend, vin)

    arrived(got_yg)
    gates = nn(nlow[...], weight(GAT, 512))
    gated[...], dgel[...] = gelu_parts(gates)

    taps = wb[group, :, :, :, EXT:UPA].reshape(128, 256)
    lane = lax.broadcasted_iota(jnp.int32, (128, 256), 1)
    share = jnp.where(lane < TAPS, 1.0 / (1 << (lane >> 5)).astype(F32), 0.0)
    squares = taps.astype(F32) * taps.astype(F32) * share
    high = squares.astype(BF16)
    rest = (squares - high.astype(F32)).astype(BF16)
    ones = jnp.ones((8, 256), BF16)
    norm = lax.rsqrt((nt(ones, high) + nt(ones, rest))[0:1] + EPSILON)
    loads[0].wait()
    for i in range(4):
        part = pl.ds(512 * i, 512)
        spec_k[part, :] = nt(rep[part, :], taps) * norm

    def spectrum(src, dst):
        signal = src[...].reshape(SLOT, 128)

        def step(i, carry):
            part = pl.ds(pl.multiple_of(i * 256, 256), 256)
            dst[part, :] = nn(dft[part, :], signal)
            return carry

        lax.fori_loop(0, 8, step, 0)

    def back(dst):
        def step(i, carry):
            rows_of = inv[pl.ds(pl.multiple_of(i * 256, 256), 256), :]
            dst[pl.ds(i * 4, 4)] = nn(rows_of, spec_y[...]).astype(BF16).reshape(4, 64, 128)
            return carry

        lax.fori_loop(0, 2, step, 0)

    loads[1].wait()
    loads[2].wait()
    arrived(got_v)
    spectrum(vin, spec_v)
    for i in range(4):
        re, im = pl.ds(256 * i, 256), pl.ds(SLOT + 256 * i, 256)
        kr, ki, vr, vi = spec_k[re, :], spec_k[im, :], spec_v[re, :], spec_v[im, :]
        spec_y[re, :] = (kr * vr - ki * vi).astype(BF16)
        spec_y[im, :] = (kr * vi + ki * vr).astype(BF16)
    back(ysend)
    sent_c, got_c = give_back(ysend, cin)

    arrived(got_xu)
    got_xu = to_sibling(XU)
    arrived(got_yu)
    got_yu = to_sibling(YU)
    arrived(got_dz)
    got_dc = [push(wd.at[:, c], wd.at[:, c], sibling)]
    gmo[...] = (cot_ref[...] * mask).astype(BF16)
    arrived(got_xu)
    arrived(got_yu)
    arrived(got_dc)
    for f in range(4):
        gact[:, 512 * f : 512 * f + 512] = nt(gmo[...], wd[f].reshape(512, 512))

    def whole(ref):
        lines = [jnp.concatenate([ref[4 * b + g] for g in range(4)], axis=1) for b in range(2)]
        return jnp.concatenate(lines, axis=0).astype(F32)

    taken_back(got_c)
    mixed[...] = whole(cin) + skip * val[...]
    bi[...] = (mixed[...] * gated[...]).astype(BF16)
    hidden = x_ref[...] + mask * nn(bi[...], weight(OUT, 512))
    hid[...] = hidden
    centered = hidden - jnp.mean(hidden, axis=1, keepdims=True)
    inv_two = lax.rsqrt(jnp.mean(centered * centered, axis=1, keepdims=True) + EPSILON)
    xh2[...] = centered * inv_two
    n2l[...] = (xh2[...] * gain_two).astype(BF16)
    up_at = (UPA, UPA + 512, UPB, UPB + 512)
    grad_n2 = jnp.zeros((128, 512), F32)
    for f in range(4):
        part = slice(512 * f, 512 * f + 512)
        w_up = weight(up_at[f], 512)
        gelu, slope = gelu_parts(nn(n2l[...], w_up))
        act[:, part] = gelu.astype(BF16)
        gup[:, part] = (gact[:, part] * slope).astype(BF16)
        grad_n2 = grad_n2 + nt(gup[:, part], w_up)
    weighted = gain_two * grad_n2
    mean_one = jnp.mean(weighted, axis=1, keepdims=True)
    mean_two = jnp.mean(weighted * xh2[...], axis=1, keepdims=True)
    grad_hidden = cot_ref[...] + (weighted - mean_one - xh2[...] * mean_two) * inv_two
    ghid[...] = grad_hidden
    gb[...] = (mask * grad_hidden).astype(BF16)
    grad_bi = nt(gb[...], weight(OUT, 512))
    grad_mixed = grad_bi * gated[...]
    low = grad_mixed.astype(BF16)
    for b in range(2):
        for g in range(4):
            gsend[4 * b + g] = low[64 * b : 64 * b + 64, 128 * g : 128 * g + 128]
    got_g = scatter(gsend, gvin)

    prods[0:128] = (grad_n2 * xh2[...]).astype(BF16)
    prods[128:256] = (grad_mixed * val[...]).astype(BF16)
    ggate[...] = (grad_bi * mixed[...] * dgel[...]).astype(BF16)
    val[...] = skip * grad_mixed

    mine = c == 0

    def split(grad, first, width):
        grad = grad.reshape(4, 2, 4, 16, width)
        at = slice(first, first + width)
        acc[:, :, :, at] = jnp.where(mine, grad[:, 0], grad[:, 1])
        csw[:, :, :, at] = jnp.where(mine, grad[:, 1], grad[:, 0]).astype(BF16)

    def swap_cores(p):
        return [push(csw.at[:, :, :, cols(p)], crw.at[:, :, :, cols(p)], sibling)]

    split(tn(n2l[...], gup[:, 0:512]), UPA, 512)
    split(tn(n2l[...], gup[:, 512:1024]), UPA + 512, 512)
    rs_xu = swap_cores(XU)
    split(tn(n2l[...], gup[:, 1024:1536]), UPB, 512)
    split(tn(n2l[...], gup[:, 1536:2048]), UPB + 512, 512)
    rs_yu = swap_cores(YU)
    for f in range(4):
        grad = tn(act[:, 512 * f : 512 * f + 512], gmo[...]).reshape(2, 4, 4, 16, 512)
        accd[f] = jnp.where(mine, grad[0], grad[1])
        csd[f] = jnp.where(mine, grad[1], grad[0]).astype(BF16)
    rs_d = [push(csd, crd, sibling)]
    split(tn(nlow[...], ggate[...]), GAT, 512)
    split(tn(bi[...], gb[...]), OUT, 512)
    rs_yg = swap_cores(YG)

    def reduce_bulk_x(p, got):
        at = slice(*p)
        arrived(got)
        for k in range(4):
            total = acc[k, :, :, at] + crw[k, :, :, at].astype(F32)
            acc[k, :, :, at] = total
            s2[k, :, :, at] = total.astype(BF16)
        return ring(
            x, x_at, lambda to: s2.at[to, :, :, cols(p)], lambda i: r2.at[i - 1, :, :, cols(p)]
        )

    def reduce_bulk_y(p, got):
        at = slice(*p)
        arrived(got)
        for k in range(4):
            total = acc[k, :, :, at] + crw[k, :, :, at].astype(F32)
            acc[k, :, :, at] = total
            s2[k, :, :, at] = total.astype(BF16)
        return ring(
            y, y_at, lambda to: s2.at[:, to, :, cols(p)], lambda i: r2.at[i - 1, :, :, cols(p)]
        )

    def reduce_next(p, got, own, me, at_device):
        at = slice(*p)
        arrived(got)
        total = own
        for k in range(3):
            total = total + r2[k, :, :, at].astype(F32)
        acc2[:, :, at] = total
        s3[:, :, at] = total.astype(BF16)
        return ring(
            me, at_device, lambda to: s3.at[to, :, cols(p)], lambda i: r3.at[i - 1, :, cols(p)]
        )

    def reduce_next_x(p, got):
        return reduce_next(p, got, acc[x, :, :, slice(*p)], y, y_at)

    def reduce_next_y(p, got):
        return reduce_next(p, got, acc[:, y, :, slice(*p)], x, x_at)

    def reduce_last(p, got, me):
        at = slice(*p)
        arrived(got)
        total = acc2[me, :, at]
        for k in range(3):
            total = total + r3[k, :, at].astype(F32)
        tail[:, at] = total

    rs_xu = reduce_bulk_x(XU, rs_xu)
    rs_yu = reduce_bulk_y(YU, rs_yu)
    arrived(rs_d)
    for k in range(4):
        total = accd[k] + crd[k].astype(F32)
        accd[k] = total
        s2d[k] = total.astype(BF16)
    rs_d = ring(z, z_at, lambda to: s2d.at[:, :, to], lambda i: r2d.at[i - 1])

    mlp_out = jnp.zeros((128, 512), F32)
    for f in range(4):
        mlp_out = mlp_out + nn(act[:, 512 * f : 512 * f + 512], wd[f].reshape(512, 512))
    out_ref[...] = hid[...] + mask * mlp_out

    arrived(got_g)
    spectrum(gvin, spec_g)
    for i in range(4):
        re, im = pl.ds(256 * i, 256), pl.ds(SLOT + 256 * i, 256)
        kr, ki, gr, gi = spec_k[re, :], spec_k[im, :], spec_g[re, :], spec_g[im, :]
        spec_y[re, :] = (kr * gr + ki * gi).astype(BF16)
        spec_y[im, :] = (kr * gi - ki * gr).astype(BF16)
    back(csend)
    sent_g, got_gc = give_back(csend, gcin)

    rs_yg = reduce_bulk_y(YG, rs_yg)

    re = pl.ds(pl.multiple_of(half * 512, 512), 512)
    im = pl.ds(pl.multiple_of(half * 512 + SLOT, 512), 512)
    vr, vi, gr, gi = spec_v[re, :], spec_v[im, :], spec_g[re, :], spec_g[im, :]
    tap_grad = tn((vr * gr + vi * gi).astype(BF16), rep[re, :])
    tap_grad = (tap_grad + tn((vr * gi - vi * gr).astype(BF16), rep[im, :])) * (1.0 / SLOT)

    rs_xu = reduce_next_x(XU, rs_xu)
    rs_yu = reduce_next_y(YU, rs_yu)

    taken_back(got_gc)
    grad_val = (whole(gcin) + val[...]).astype(BF16)
    grad_normed = nt(grad_val, weight(VAL, 512)) + nt(ggate[...], weight(GAT, 512))
    prods[256:384] = (grad_normed * xh1[...]).astype(BF16)
    owner = lax.broadcasted_iota(jnp.int32, (384, 256), 0) >> 7
    column = lax.broadcasted_iota(jnp.int32, (384, 256), 1)
    wanted = jnp.where(owner == 2, TAPS, TAPS + 1 + owner)
    sums = tn(prods[...], jnp.where(column == wanted, 1.0, 0.0).astype(BF16))
    parts = [
        sums[128 * k : 128 * k + 128] + tap_grad * jnp.where(group == k, 1.0, 0.0) for k in range(4)
    ]
    split(jnp.concatenate(parts, axis=0), EXT, 256)
    split(tn(nlow[...], grad_val), VAL, 512)
    rs_xe = swap_cores(XE)

    weighted = gain_one * grad_normed
    mean_one = jnp.mean(weighted, axis=1, keepdims=True)
    mean_two = jnp.mean(weighted * xh1[...], axis=1, keepdims=True)
    gin_ref[...] = ghid[...] + (weighted - mean_one - xh1[...] * mean_two) * inv1[...]

    rs_xe = reduce_bulk_x(XE, rs_xe)
    rs_yg = reduce_next_y(YG, rs_yg)
    arrived(rs_d)
    total = accd[:, :, z]
    for k in range(3):
        total = total + r2d[k].astype(F32)
    acc2d[...] = total
    s3d[...] = total.astype(BF16)
    rs_d = ring(y, y_at, lambda to: s3d.at[:, to], lambda i: r3d.at[i - 1])
    reduce_last(XU, rs_xu, y)
    reduce_last(YU, rs_yu, x)
    rs_xe = reduce_next_x(XE, rs_xe)
    reduce_last(YG, rs_yg, x)
    arrived(rs_d)
    total = acc2d[:, y]
    for k in range(3):
        total = total + r3d[k].astype(F32)
    acc3d[...] = total
    s4d[...] = total.astype(BF16)
    rs_d = ring(x, x_at, lambda to: s4d.at[to], lambda i: r4d.at[i - 1])
    reduce_last(XE, rs_xe, y)
    tail[:, END:WIDE] = jnp.zeros((16, WIDE - END), F32)
    stacked = jnp.concatenate(
        [tail[:, 1024 * u : 1024 * u + 1024].astype(BF16) for u in range(4)], axis=0
    )
    s4[...] = nn(swap, stacked).astype(BF16).reshape(4, 16, 1024)
    rs_z = ring(z, z_at, lambda to: s4.at[to], lambda i: r4.at[i - 1])
    arrived(rs_d)
    total = acc3d[x]
    for k in range(3):
        total = total + r4d[k].astype(F32)
    gdown_ref[...] = total
    arrived(rs_z)
    total = s4[z].astype(F32)
    for k in range(3):
        total = total + r4[k].astype(F32)
    gpack_ref[...] = total

    for copy in started:
        if copy is not None:
            copy.wait_send()
    sent_back(sent_c)
    sent_back(sent_g)


def scratch():
    def f32(*shape):
        return pltpu.VMEM(shape, F32)

    def b16(*shape):
        return pltpu.VMEM(shape, BF16)

    copies = 160
    return [
        b16(4, 16, 1024), b16(4, 2, 4, 16, WIDE), b16(4, 2, 4, 4, 16, 512),
        b16(2 * SLOT, SLOT), b16(512, 2 * SLOT), b16(2 * SLOT, 256),
        f32(128, 512), f32(128, 1), b16(128, 512), f32(128, 512), f32(128, 512), f32(128, 512), f32(128, 512),
        b16(128, 512), f32(128, 512), f32(128, 512), b16(128, 512),
        b16(128, 512), f32(128, FF), b16(128, FF), b16(128, FF), f32(128, 512), b16(128, 512), b16(128, 512),
        b16(384, 512),
        b16(8, 64, 128), b16(16, 64, 128), b16(8, 64, 128), b16(8, 64, 128),
        b16(8, 64, 128), b16(16, 64, 128), b16(8, 64, 128), b16(8, 64, 128),
        f32(2 * SLOT, 128), f32(2 * SLOT, 128), f32(2 * SLOT, 128), b16(2 * SLOT, 128),
        f32(4, 4, 16, WIDE), b16(4, 4, 16, WIDE), b16(4, 4, 16, WIDE), b16(4, 4, 16, WIDE), b16(3, 4, 16, WIDE),
        f32(4, 16, WIDE), b16(4, 16, WIDE), b16(3, 16, WIDE), f32(16, WIDE),
        f32(4, 4, 4, 16, 512), b16(4, 4, 4, 16, 512), b16(4, 4, 4, 16, 512), b16(4, 4, 4, 16, 512),
        b16(3, 4, 4, 16, 512), f32(4, 4, 16, 512), b16(4, 4, 16, 512), b16(3, 4, 16, 512),
        f32(4, 16, 512), b16(4, 16, 512), b16(3, 16, 512),
        b16(4, 16, 1024), b16(3, 16, 1024),
        pltpu.SemaphoreType.DMA((copies,)), pltpu.SemaphoreType.DMA((copies,)), pltpu.SemaphoreType.DMA((3,)),
    ]


def body(
    inputs,
    cotangent,
    lengths,
    gain_first,
    proj_in,
    sub_kernels,
    skip_gain,
    proj_out,
    gain_second,
    mlp_up,
    mlp_down,
):
    forward, inverse, repeat = transforms()
    taps = sub_kernels.reshape(TAPS, 4).T
    extras = jnp.concatenate(
        [
            taps,
            gain_first[:, None],
            gain_second[:, None],
            skip_gain[:, None],
            jnp.zeros((4, 256 - TAPS - 3), BF16),
        ],
        axis=1,
    )
    pack = jnp.concatenate(
        [
            proj_in[:, :D],
            extras,
            mlp_up[:, :1024],
            proj_in[:, D:],
            proj_out,
            mlp_up[:, 1024:],
            jnp.zeros((4, WIDE - END), BF16),
        ],
        axis=1,
    )
    pack = pack.reshape(4, 4, 1024).transpose(1, 0, 2).reshape(16, 1024)

    vmem = pl.BlockSpec(memory_space=pltpu.VMEM)
    smem = pl.BlockSpec(memory_space=pltpu.SMEM)
    anywhere = pl.BlockSpec(memory_space=pl.ANY)
    outputs, grad_inputs, gpack, gdown = pl.pallas_call(
        fused,
        out_shape=(
            jax.ShapeDtypeStruct((128, 512), F32),
            jax.ShapeDtypeStruct((128, 512), F32),
            jax.ShapeDtypeStruct((16, 1024), F32),
            jax.ShapeDtypeStruct((16, 512), F32),
        ),
        in_specs=[vmem, vmem, smem, vmem, vmem, anywhere, anywhere, anywhere],
        out_specs=(vmem, vmem, vmem, vmem),
        scratch_shapes=scratch(),
        compiler_params=pltpu.CompilerParams(
            collective_id=0, has_side_effects=True, vmem_limit_bytes=60 * 2**20
        ),
        name="block",
    )(
        inputs.reshape(128, 512),
        cotangent.reshape(128, 512),
        lengths,
        pack,
        mlp_down,
        jnp.asarray(forward),
        jnp.asarray(inverse),
        jnp.asarray(repeat),
    )
    rows = gpack.reshape(4, 4, 1024).transpose(1, 0, 2).reshape(4, WIDE)
    grad_taps = rows[:, EXT : EXT + TAPS]
    share = jnp.asarray(np.repeat(0.5 ** np.arange(NSUB), SUBTAPS).astype(np.float32))[None, :]
    low_taps = taps.astype(F32)
    norm = lax.rsqrt(jnp.sum(low_taps * low_taps * share, axis=1, keepdims=True) + EPSILON)
    along = jnp.sum(low_taps * grad_taps, axis=1, keepdims=True)
    grad_sub = norm * grad_taps - share * low_taps * (norm * norm * norm * along)
    return (
        outputs.reshape(2, 64, 512),
        grad_inputs.reshape(2, 64, 512),
        rows[:, EXT + TAPS],
        jnp.concatenate([rows[:, VAL:EXT], rows[:, GAT:OUT]], axis=1),
        grad_sub.T.reshape(NSUB, SUBTAPS, 4),
        rows[:, EXT + TAPS + 2],
        rows[:, OUT:UPB],
        rows[:, EXT + TAPS + 1],
        jnp.concatenate([rows[:, UPA:GAT], rows[:, UPB:END]], axis=1),
        gdown,
    )


def solution(mesh):
    in_specs = (
        P("dp", "seq", None),
        P("dp", "seq", None),
        P("dp"),
        P(("dp", "seq")),
        P(("dp", "seq"), None),
        P(None, None, ("dp", "seq")),
        P(("dp", "seq")),
        P(("dp", "seq"), None),
        P(("dp", "seq")),
        P(("dp", "seq"), None),
        P(("dp", "seq"), None),
    )
    out_specs = (
        P("dp", "seq", None),
        P("dp", "seq", None),
        P(("dp", "seq")),
        P(("dp", "seq"), None),
        P(None, None, ("dp", "seq")),
        P(("dp", "seq")),
        P(("dp", "seq"), None),
        P(("dp", "seq")),
        P(("dp", "seq"), None),
        P(("dp", "seq"), None),
    )
    return jax.shard_map(body, mesh=mesh, in_specs=in_specs, out_specs=out_specs, check_vma=False)
```

time: 3670 us -> 106 us (0.03)
  local copies, waits for them, and re-layouts: 1430 us -> 13.5 us
  waiting for transfers between devices: 1360 us -> 0 us
  matrix products: 371 us -> 0 us
  blocking collectives: 269 us -> 0 us
  other arithmetic: 135 us -> 1.47 us
  Pallas kernels: 0 us -> 90 us
  starting transfers between devices: 66.5 us -> 0 us
    reduce_scatter x2 -> x0, waiting for transfers between devices: 1200 us -> none  [the longest x1 642 us: body(): lax.psum_scatter(grad_down, ('dp', 'seq'), scatter_dimension=0, tiled=True)]
    gather x62 -> x0, local copies, waits for them, and re-layouts: 939 us -> none  [toeplitz_block(): return jnp.take(window, tap_index, axis=0)]
    dot_general x60 -> x0, matrix products: 371 us -> none  [the longest x16 131 us: apply_block(): jnp.einsum('abc,sbc->sac', toeplitz, source, preferred_element_type=jnp.f...]
    transpose x16 -> x0, local copies, waits for them, and re-layouts: 248 us -> none  [block_grads(): jnp.einsum('sac,sbc->abc', grad_out, reversed_in, preferred_element_type=...]
    unnamed x7 -> x0, waiting for transfers between devices: 162 us -> none
    unnamed x2 -> x0, blocking collectives: 157 us -> none
    reshape x18 -> x4, local copies, waits for them, and re-layouts: 154 us -> 1.66 us  [the longest x1 0.86 us: body(): rows = gpack.reshape(4, 4, 1024).transpose(1, 0, 2).reshape(4, WIDE)]
    all_gather x2 -> x0, blocking collectives: 113 us -> none  [the longest x1 61.6 us: body(): lax.all_gather(sub_kernels, ('dp', 'seq'), axis=2, tiled=True)]
  transfers between devices with their start and end apart: 36 -> 0, of which waited for: 3 -> 0; matrix products, arithmetic and copies ran while one was open for 32% -> 0% of each run, Pallas kernels for 0% -> 0%
where the time goes in v1:
time: 106 us
  Pallas kernels  90 us (85%)
  local copies, waits for them, and re-layouts  13.5 us (13%)
  other arithmetic  1.47 us (1%)
    pallas_call x1, Pallas kernels, body(): pl.pallas_call(fused, out_shape=(jax.ShapeDtypeStruct((128, 512), F32), j...  90 us
    unnamed x7, local copies, waits for them, and re-layouts  6.02 us

profile of v1, /device:TPU:0, one launch (start us, length us, event | category | flops | bytes accessed | tf_op | source)
XLA Modules:
  0.0 105.6 jit_solution(4862930473373264032)
XLA Ops:
  0.6 0.8 copy.38
  1.4 0.8 copy.40
  2.2 0.8 copy.39
  2.9 0.7 copy.37
  3.6 0.1 reshape.69
  3.7 0.7 fusion.10
  4.4 0.7 fusion.9
  5.1 0.8 concatenate.9
  5.9 0.6 reshape.71.pack_ref
  6.6 0.0 copy-start
  6.6 90.0 %block.1 = (f32[128,512]{1,0:T(8,128)}, f32[128,512]{1,0:T(8,128)}, f32[16,1024]{1,0:T(8,128)}, f32[16,512]{1,0:T(8,128)}) custom-call(f32[128,512]{1,0:T(8,128)} %bitcast.28, f32[128,512]{1,0:T(8,128)} %bitcast.29, s32[2]{0:T(128)} %len_ref.1, bf16[16,1024]{1,0:T(8,128)(2,1)} %reshape.71.pack_ref, bf16[16,512]{1,0:T(8,128)(2,1)} %down_ref.1, ...), custom_call_target="tpu_custom_call" | custom-call | tf_op jit(solution)/shard_map/block/pallas_call | solution.py:624
  96.5 0.9 reshape.74
  97.4 0.0 copy-done
  97.4 0.1 fusion.1
  97.6 0.1 fusion.4
  97.7 0.7 slice_reduce_fusion
  98.4 0.1 reshape.76
  98.5 0.6 copy.42
  99.1 0.6 fusion.8
  99.7 0.6 pad_maximum_fusion
  100.3 0.6 pad_maximum_fusion.1
  100.9 1.7 %copy.46 = f32[2,64,512]{2,1,0:T(8,128)} copy(f32[2,64,512]{2,1,0:T(8,128)} %bitcast.31) | data formatting | bytes 524288
  102.6 1.7 %copy.47 = f32[2,64,512]{2,1,0:T(8,128)} copy(f32[2,64,512]{2,1,0:T(8,128)} %bitcast.30) | data formatting | bytes 524288
  104.3 1.4 %copy.48 = f32[16,512]{1,0:T(8,128)} copy(f32[16,512]{1,0:T(8,128)} %get-tuple-element.73) | data formatting | bytes 65536
  (4 shorter events, 0.0 us)
Async XLA Ops:
  6.6 90.9 %copy-start = (f32[160]{0:T(256)S(1)}, f32[160]{0:T(256)}, u32[]{:S(2)}) copy-start(f32[160]{0:T(256)} %constant.18.clone) | copy-start | bytes 1924

commit v2 on v1

v2 whole, which is shorter than its diff:
```python
import math

import jax
import jax.numpy as jnp
import ml_dtypes
import numpy as np
from jax import lax
from jax.experimental import pallas as pl
from jax.experimental.pallas import tpu as pltpu
from jax.sharding import PartitionSpec as P

EPSILON = 1e-05
D = 512
FF = 2048
SLOT = 1024
NSUB = 5
SUBTAPS = 32
TAPS = NSUB * SUBTAPS
F32 = jnp.float32
BF16 = jnp.bfloat16
MESH = pl.DeviceIdType.MESH

VAL, EXT, END, UPA, GAT, OUT, UPB, WIDE = 0, 512, 768, 1024, 2048, 2560, 3072, 4096
XE, YE, XR, YR, EARLY = (VAL, 384), (384, END), (UPA, UPB), (UPB, WIDE), (VAL, END)
X1, X2 = (UPA, GAT), (GAT, UPB)
ZD, YD = (0, 384), (384, 512)


def transforms():
    place = np.arange(SLOT)
    angle = 2 * np.pi * ((2 * place[:, None] + 1) * place[None, :] % (4 * SLOT)) / (4 * SLOT)
    forward = np.concatenate([np.cos(angle), -np.sin(angle)], axis=0)
    inverse = forward.T / SLOT
    repeat = np.zeros((SLOT, 256))
    first = 0
    for octave in range(NSUB):
        for tap in range(SUBTAPS):
            repeat[first : first + 2**octave, octave * SUBTAPS + tap] = 0.5**octave
            first += 2**octave
    half = np.stack([inverse[:512], inverse[512:]])
    return tuple(a.astype(ml_dtypes.bfloat16) for a in (forward, half, forward @ repeat))


def nn(a, b):
    return lax.dot_general(a, b, (((1,), (0,)), ((), ())), preferred_element_type=F32)


def nt(a, b):
    return lax.dot_general(a, b, (((1,), (1,)), ((), ())), preferred_element_type=F32)


def tn(a, b):
    return lax.dot_general(a, b, (((0,), (0,)), ((), ())), preferred_element_type=F32)


def gelu_parts(v):
    cdf = 0.5 * (1.0 + lax.erf(v * math.sqrt(0.5)))
    slope = cdf + v * (jnp.exp(-0.5 * v * v) * (1.0 / math.sqrt(2 * math.pi)))
    return v * cdf, slope


def swap_matrix():
    row = lax.broadcasted_iota(jnp.int32, (64, 64), 0)
    col = lax.broadcasted_iota(jnp.int32, (64, 64), 1)
    source = ((row >> 2) & 3) * 16 + (row >> 4) * 4 + (row & 3)
    return jnp.where(col == source, 1.0, 0.0).astype(BF16)


def fused(
    x_hbm, cot_hbm, len_ref, gain_one_hbm, gain_two_hbm, skip_hbm, in_hbm, sub_hbm, mix_hbm, up_hbm, down_hbm,
    dft_hbm, inv_hbm, rep_hbm,
    out_hbm, gin_hbm, gearly_ref, grest_ref, gdown_ref,
    xin, cot, outv, ginv, gain_one_ref, gain_two_ref, skip_ref, in_ref, sub_ref, mix_ref, up_ref, down_ref,
    zearly, zrest, wb, wd, dft, inv, rep,
    xh1, inv1, nlow, val, gated, dgel, mixed, bi, hid, xh2, n2l, gmo, gact, act, gup, ghid, gb, ggate,
    vsend, vin, ysend, cin, gsend, gvin, csend, gcin, nls, nin, spec_v, spec_k, spec_g, spec_y,
    n2t, nlt, bit, act_t, nint,
    acc, csw, crw, s2, r2, acc2, s3, r3, tail,
    accd, csd, crd, s2d, r2a, r2c, acc2a, s3a, r3a, acc2c, s3c, r3c, acc3d, s4d, r4d,
    ta, tcs, tcr, ts2, tr2, tacc, ts3, tr3, s4e, r4e, s4r, r4r,
    send_sem, recv_sem, local_sem,
):
    dp, j = lax.axis_index("dp"), lax.axis_index("seq")
    x, c = dp // 2, dp % 2
    y, z = j // 4, j % 4
    half, pair = j % 2, j // 2
    group = pair % 4

    def turn(v, by):
        return lax.rem(v + by, 4)

    def x_at(v):
        return (v * 2 + c, j)

    def y_at(v):
        return (dp, v * 4 + z)

    def z_at(v):
        return (dp, y * 4 + v)

    sibling = (x * 2 + 1 - c, j)

    barrier = pltpu.get_barrier_semaphore()
    partners = [sibling] + [x_at(turn(x, i)) for i in (1, 2, 3)]
    partners += [(dp, lax.rem(j + i, 16)) for i in range(1, 16)]
    for partner in partners:
        pl.semaphore_signal(barrier, inc=1, device_id=partner, device_id_type=MESH)

    small = [
        pltpu.make_async_copy(src, dst, local_sem.at[8 + k])
        for k, (src, dst) in enumerate((
            (in_hbm, in_ref), (sub_hbm, sub_ref), (gain_one_hbm, gain_one_ref), (gain_two_hbm, gain_two_ref),
            (skip_hbm, skip_ref), (up_hbm, up_ref), (mix_hbm, mix_ref), (down_hbm, down_ref),
        ))
    ]
    loads = [
        pltpu.make_async_copy(x_hbm, xin, local_sem.at[0]),
        pltpu.make_async_copy(cot_hbm, cot, local_sem.at[1]),
        pltpu.make_async_copy(rep_hbm, rep, local_sem.at[2]),
        pltpu.make_async_copy(dft_hbm, dft, local_sem.at[3]),
        pltpu.make_async_copy(inv_hbm.at[half], inv, local_sem.at[4]),
    ]
    for load in small + loads:
        load.start()
    for load in small:
        load.wait()

    lane = lax.broadcasted_iota(jnp.int32, (4, 256), 1)
    extras = jnp.zeros((4, 256), F32)
    for octave in range(NSUB):
        place = lax.broadcasted_iota(jnp.int32, (SUBTAPS, 256), 0) + SUBTAPS * octave
        spread = place == lax.broadcasted_iota(jnp.int32, (SUBTAPS, 256), 1)
        extras = extras + nn(sub_ref[octave], jnp.where(spread, 1.0, 0.0).astype(BF16))
    diagonal = lax.broadcasted_iota(jnp.int32, (4, 4), 0) == lax.broadcasted_iota(jnp.int32, (4, 4), 1)
    for k, ref in enumerate((gain_one_ref, gain_two_ref, skip_ref)):
        column = jnp.sum(jnp.where(diagonal, ref[...].astype(F32), 0.0), axis=1, keepdims=True)
        extras = jnp.where(lane == TAPS + k, column, extras)
    w_in, w_up = in_ref[...].astype(F32), up_ref[...].astype(F32)
    early = [w_in[:, 0:256], w_in[:, 256:512], extras, jnp.zeros((4, 256), F32)]
    zearly[z] = jnp.concatenate(early, axis=0).astype(BF16)
    rest = [
        w_up[:, 0:768],
        jnp.concatenate([w_up[:, 768:1024], w_in[:, 512:1024]], axis=1),
        jnp.concatenate([mix_ref[...].astype(F32), w_up[:, 1024:1280]], axis=1),
        w_up[:, 1280:2048],
    ]
    zrest[z] = jnp.concatenate(rest, axis=0).astype(BF16)
    wd[x, c, y, z] = down_ref[...]
    swap = swap_matrix()

    pl.semaphore_wait(barrier, len(partners))

    started = []

    def push(src, dst, device):
        at = len(started)
        copy = pltpu.make_async_remote_copy(
            src_ref=src,
            dst_ref=dst,
            send_sem=send_sem.at[at],
            recv_sem=recv_sem.at[at],
            device_id=device,
            device_id_type=MESH,
        )
        copy.start()
        started.append(copy)
        return copy

    def ring(me, at, src, dst):
        return [push(src(turn(me, i)), dst(i), at(turn(me, i))) for i in (1, 2, 3)]

    def arrived(copies):
        for copy in copies:
            copy.wait_recv()

    def same(me, at, ref):
        return ring(me, at, lambda to: ref, lambda i: ref)

    def cols(ends):
        return pl.ds(ends[0], ends[1] - ends[0])

    got_z = same(z, z_at, zearly.at[z])
    got_zr = same(z, z_at, zrest.at[z])
    got_d = same(x, x_at, wd.at[x, c, y, z])

    def first_x(p):
        return same(y, y_at, wb.at[x, c, y, :, cols(p)])

    def first_y(p):
        return same(x, x_at, wb.at[x, c, y, :, cols(p)])

    def bulk_x(p):
        return same(x, x_at, wb.at[x, c, :, :, cols(p)])

    def bulk_y(p):
        return same(y, y_at, wb.at[:, c, y, :, cols(p)])

    def to_sibling(p):
        ref = wb.at[:, c, :, :, cols(p)]
        return [push(ref, ref, sibling)]

    arrived(got_z)
    rows = nn(swap, zearly[...].reshape(64, 256)).astype(BF16)
    for q in range(3):
        wb[x, c, y, :, 256 * q : 256 * (q + 1)] = rows[16 * q : 16 * q + 16]
    got_xe, got_ye = first_x(XE), first_y(YE)

    loads[0].wait()
    source = xin[...]
    centered = source - jnp.mean(source, axis=1, keepdims=True)
    inv_one = lax.rsqrt(jnp.mean(centered * centered, axis=1, keepdims=True) + EPSILON)
    inv1[...] = inv_one
    xh1[...] = centered * inv_one

    row = lax.broadcasted_iota(jnp.int32, (128, 1), 0)
    limit = jnp.where(row < 64, len_ref[0], len_ref[1])
    mask = jnp.where((row & 63) + j * 64 < limit, 1.0, 0.0)

    arrived(got_zr)
    rows = nn(swap, zrest[...].reshape(64, 768)).astype(BF16)
    for q in range(4):
        wb[x, c, y, :, UPA + 768 * q : UPA + 768 * (q + 1)] = rows[16 * q : 16 * q + 16]

    arrived(got_xe)
    arrived(got_ye)
    got_xe, got_ye = bulk_x(XE), bulk_y(YE)
    got_xr, got_yr = first_x(XR), first_y(YR)
    arrived(got_d)
    got_zd = same(y, y_at, wd.at[:, c, y, z, :, cols(ZD)])
    got_yd = same(z, z_at, wd.at[:, c, y, z, :, cols(YD)])
    arrived(got_xe)
    arrived(got_ye)
    got_e = to_sibling(EARLY)
    arrived(got_xr)
    got_xr = bulk_x(XR)

    def weight(first, width):
        return wb[:, :, :, :, first : first + width].reshape(512, width)

    arrived(got_e)
    pick = jnp.where(
        lax.broadcasted_iota(jnp.int32, (8, 128), 1)
        == lax.broadcasted_iota(jnp.int32, (8, 128), 0) + (TAPS - 128),
        1.0,
        0.0,
    ).astype(BF16)
    gains = nt(pick, weight(EXT + 128, 128))
    gain_one, gain_two, skip = gains[0:1], gains[1:2], gains[2:3]
    nlow[...] = (xh1[...] * gain_one).astype(BF16)
    nls[...] = nlow[...].reshape(2, 64, 512)
    values = nn(nlow[...], weight(VAL, 512))
    val[...] = values
    low = values.astype(BF16)
    for b in range(2):
        for g in range(4):
            vsend[4 * b + g] = low[64 * b : 64 * b + 64, 128 * g : 128 * g + 128]

    def scatter(src, dst):
        copies = []
        for i in range(1, 16):
            to = lax.rem(j + i, 16)
            copies.append(push(src.at[to // 2], dst.at[j], (dp, to)))
        dst[j] = src[pair]
        return copies

    def eight(src, dst, target, slot, sender, own):
        base = len(started)
        copies, receipts = [], []
        for i in range(8):
            to = target(i)
            copy = pltpu.make_async_remote_copy(
                src_ref=src(i),
                dst_ref=dst.at[slot],
                send_sem=send_sem.at[base + i],
                recv_sem=recv_sem.at[base + slot],
                device_id=(dp, to),
                device_id_type=MESH,
            )

            @pl.when(to != j)
            def _(copy=copy):
                copy.start()

            @pl.when(to == j)
            def _(i=i):
                dst[slot] = own(i)

            copies.append((copy, to))
            started.append(None)
        for i in range(8):
            receipt = pltpu.make_async_remote_copy(
                src_ref=src(i),
                dst_ref=dst.at[i],
                send_sem=send_sem.at[base + i],
                recv_sem=recv_sem.at[base + i],
                device_id=sibling,
                device_id_type=MESH,
            )
            receipts.append((receipt, sender(i)))
        return copies, receipts

    def give_back(src, dst):
        return eight(
            lambda i: src.at[i], dst, lambda i: 8 * half + i, pair, lambda q: 2 * q + j // 8, lambda i: src[i]
        )

    def taken_back(receipts):
        for receipt, sender in receipts:

            @pl.when(sender != j)
            def _(receipt=receipt):
                receipt.wait_recv()

    def sent_back(copies):
        for copy, to in copies:

            @pl.when(to != j)
            def _(copy=copy):
                copy.wait_send()

    got_v = scatter(vsend, vin)
    arrived(got_yr)
    got_yr = bulk_y(YR)
    arrived(got_zd)
    got_zd = same(z, z_at, wd.at[:, c, :, z, :, cols(ZD)])
    arrived(got_yd)
    got_yd = same(y, y_at, wd.at[:, c, y, :, :, cols(YD)])

    taps = wb[group, :, :, :, EXT:END].reshape(128, 256)
    skip_group = nt(pick, taps[:, 128:256])[2:3]
    lane = lax.broadcasted_iota(jnp.int32, (128, 256), 1)
    share = jnp.where(lane < TAPS, 1.0 / (1 << (lane >> 5)).astype(F32), 0.0)
    squares = taps.astype(F32) * taps.astype(F32) * share
    high = squares.astype(BF16)
    rest = (squares - high.astype(F32)).astype(BF16)
    ones = jnp.ones((8, 256), BF16)
    norm = lax.rsqrt((nt(ones, high) + nt(ones, rest))[0:1] + EPSILON)
    loads[2].wait()
    for i in range(4):
        part = pl.ds(512 * i, 512)
        spec_k[part, :] = nt(rep[part, :], taps) * norm

    def spectrum(src, dst):
        signal = src[...].reshape(SLOT, 128)

        def step(i, carry):
            part = pl.ds(pl.multiple_of(i * 256, 256), 256)
            dst[part, :] = nn(dft[part, :], signal)
            return carry

        lax.fori_loop(0, 8, step, 0)

    def back(dst, more=None):
        def step(i, carry):
            part = nn(inv[pl.ds(pl.multiple_of(i * 256, 256), 256), :], spec_y[...])
            if more is not None:
                part = part + more(i)
            dst[pl.ds(i * 4, 4)] = part.astype(BF16).reshape(4, 64, 128)
            return carry

        lax.fori_loop(0, 2, step, 0)

    loads[3].wait()
    loads[4].wait()
    arrived(got_v)
    spectrum(vin, spec_v)
    for i in range(4):
        re, im = pl.ds(256 * i, 256), pl.ds(SLOT + 256 * i, 256)
        kr, ki, vr, vi = spec_k[re, :], spec_k[im, :], spec_v[re, :], spec_v[im, :]
        spec_y[re, :] = (kr * vr - ki * vi).astype(BF16)
        spec_y[im, :] = (kr * vi + ki * vr).astype(BF16)
    back(ysend)
    sent_c, got_c = give_back(ysend, cin)
    sent_n, got_n = eight(
        lambda k: nls.at[k // 4], nin, lambda k: 2 * k + j // 8, j % 8, lambda i: 8 * half + i, lambda k: nls[k // 4]
    )

    arrived(got_xr)
    got_xr = to_sibling(XR)
    arrived(got_yr)
    got_yr = to_sibling(YR)
    arrived(got_zd)
    arrived(got_yd)
    got_dc = [push(wd.at[:, c], wd.at[:, c], sibling)]
    loads[1].wait()
    gmo[...] = (cot[...] * mask).astype(BF16)
    arrived(got_xr)
    gates = nn(nlow[...], weight(GAT, 512))
    gated[...], dgel[...] = gelu_parts(gates)
    arrived(got_yr)
    arrived(got_dc)
    for f in range(4):
        gact[:, 512 * f : 512 * f + 512] = nt(gmo[...], wd[f].reshape(512, 512))

    def whole(ref):
        lines = [jnp.concatenate([ref[4 * b + g] for g in range(4)], axis=1) for b in range(2)]
        return jnp.concatenate(lines, axis=0).astype(F32)

    taken_back(got_c)
    mixed[...] = whole(cin) + skip * val[...]
    bi[...] = (mixed[...] * gated[...]).astype(BF16)
    hidden = xin[...] + mask * nn(bi[...], weight(OUT, 512))
    hid[...] = hidden
    centered = hidden - jnp.mean(hidden, axis=1, keepdims=True)
    inv_two = lax.rsqrt(jnp.mean(centered * centered, axis=1, keepdims=True) + EPSILON)
    xh2[...] = centered * inv_two
    n2l[...] = (xh2[...] * gain_two).astype(BF16)
    up_at = (UPA, UPA + 512, UPB, UPB + 512)
    grad_n2 = jnp.zeros((128, 512), F32)
    for f in range(4):
        part = slice(512 * f, 512 * f + 512)
        w_up = weight(up_at[f], 512)
        gelu, slope = gelu_parts(nn(n2l[...], w_up))
        act[:, part] = gelu.astype(BF16)
        gup[:, part] = (gact[:, part] * slope).astype(BF16)
        grad_n2 = grad_n2 + nt(gup[:, part], w_up)
    weighted = gain_two * grad_n2
    mean_one = jnp.mean(weighted, axis=1, keepdims=True)
    mean_two = jnp.mean(weighted * xh2[...], axis=1, keepdims=True)
    grad_hidden = cot[...] + (weighted - mean_one - xh2[...] * mean_two) * inv_two
    ghid[...] = grad_hidden
    gb[...] = (mask * grad_hidden).astype(BF16)
    grad_bi = nt(gb[...], weight(OUT, 512))
    grad_mixed = grad_bi * gated[...]
    low = grad_mixed.astype(BF16)
    for b in range(2):
        for g in range(4):
            gsend[4 * b + g] = low[64 * b : 64 * b + 64, 128 * g : 128 * g + 128]
    got_g = scatter(gsend, gvin)

    ggate[...] = (grad_bi * mixed[...] * dgel[...]).astype(BF16)
    skip_grad = (grad_mixed * val[...]).astype(BF16)

    def turned(ref):
        return ref[...].astype(F32).T.astype(BF16)

    def grads(lhs, rhs, width, keep, send):
        own, other = lhs[:, c].reshape(-1, 128), lhs[:, 1 - c].reshape(-1, 128)
        for n in range(0, width, 256):
            keep(n, nn(own, rhs(n)))
            send(n, nn(other, rhs(n)).astype(BF16))

    def grads_wide(lhs, rhs, first, width):
        def keep(n, value):
            acc[:, :, :, first + n : first + n + 256] = value.reshape(4, 4, 16, 256)

        def send(n, value):
            csw[:, :, :, first + n : first + n + 256] = value.reshape(4, 4, 16, 256)

        grads(lhs, rhs, width, keep, send)

    def swap_cores(p):
        return [push(csw.at[:, :, :, cols(p)], crw.at[:, :, :, cols(p)], sibling)]

    def add_core(p):
        at = slice(*p)
        for k in range(4):
            total = acc[k, :, :, at] + crw[k, :, :, at].astype(F32)
            acc[k, :, :, at] = total
            s2[k, :, :, at] = total.astype(BF16)

    def reduce_bulk_x(p):
        return ring(
            x, x_at, lambda to: s2.at[to, :, :, cols(p)], lambda i: r2.at[i - 1, :, :, cols(p)]
        )

    def reduce_bulk_y(p):
        return ring(
            y, y_at, lambda to: s2.at[:, to, :, cols(p)], lambda i: r2.at[i - 1, :, :, cols(p)]
        )

    def reduce_next(p, got, own, me, at_device):
        at = slice(*p)
        arrived(got)
        total = own
        for k in range(3):
            total = total + r2[k, :, :, at].astype(F32)
        acc2[:, :, at] = total
        s3[:, :, at] = total.astype(BF16)
        return ring(
            me, at_device, lambda to: s3.at[to, :, cols(p)], lambda i: r3.at[i - 1, :, cols(p)]
        )

    def reduce_next_x(p, got):
        return reduce_next(p, got, acc[x, :, :, slice(*p)], y, y_at)

    def reduce_next_y(p, got):
        return reduce_next(p, got, acc[:, y, :, slice(*p)], x, x_at)

    def reduce_last(p, got, me):
        at = slice(*p)
        arrived(got)
        total = acc2[me, :, at]
        for k in range(3):
            total = total + r3[k, :, at].astype(F32)
        tail[:, at] = total

    def swapped(blocks):
        stacked = jnp.concatenate(blocks, axis=0).astype(BF16)
        return nn(swap, stacked).astype(BF16).reshape(4, 16, -1)

    n2t[...] = turned(n2l).reshape(4, 2, 64, 128)
    grads_wide(n2t, lambda n: gup[:, n : n + 256], UPA, 1024)
    rs_x1 = swap_cores(X1)
    act_t[...] = turned(act).reshape(4, 2, 256, 128)
    for f in range(4):
        for n in range(0, 512, 256):
            part = gmo[:, n : n + 256]
            accd[f, :, :, :, n : n + 256] = nn(act_t[f, c], part).reshape(4, 4, 16, 256)
            other = nn(act_t[f, 1 - c], part).astype(BF16)
            csd[f, :, :, :, n : n + 256] = other.reshape(4, 4, 16, 256)
    rs_d = [push(csd, crd, sibling)]
    arrived(rs_x1)
    add_core(X1)
    rs_x1 = reduce_bulk_x(X1)
    nlt[...] = turned(nlow).reshape(4, 2, 64, 128)
    grads_wide(nlt, lambda n: ggate[:, n : n + 256], GAT, 512)
    bit[...] = turned(bi).reshape(4, 2, 64, 128)
    grads_wide(bit, lambda n: gb[:, n : n + 256], OUT, 512)
    rs_x2 = swap_cores(X2)
    arrived(rs_d)
    for k in range(4):
        total = accd[k] + crd[k].astype(F32)
        accd[k] = total
        s2d[k] = total.astype(BF16)
    rs_zd = ring(
        z, z_at, lambda to: s2d.at[:, :, to, :, cols(ZD)], lambda i: r2a.at[i - 1]
    )
    rs_yd = ring(y, y_at, lambda to: s2d.at[:, to, :, :, cols(YD)], lambda i: r2c.at[i - 1])
    grads_wide(n2t, lambda n: gup[:, 1024 + n : 1280 + n], UPB, 1024)
    rs_yr = swap_cores(YR)
    arrived(rs_x2)
    add_core(X2)
    rs_x2 = reduce_bulk_x(X2)
    arrived(rs_yr)
    add_core(YR)
    rs_yr = reduce_bulk_y(YR)

    taken_back(got_n)
    nint[...] = nin[...].reshape(512, 512).astype(F32).T.astype(BF16).reshape(4, 2, 64, 512)
    arrived(got_g)
    spectrum(gvin, spec_g)
    for i in range(4):
        re, im = pl.ds(256 * i, 256), pl.ds(SLOT + 256 * i, 256)
        kr, ki, gr, gi = spec_k[re, :], spec_k[im, :], spec_g[re, :], spec_g[im, :]
        spec_y[re, :] = (kr * gr + ki * gi).astype(BF16)
        spec_y[im, :] = (kr * gi - ki * gr).astype(BF16)

    def direct(i):
        return skip_group * gvin[pl.ds(8 * half + 4 * i, 4)].reshape(256, 128).astype(F32)

    back(csend, direct)
    sent_g, got_gc = give_back(csend, gcin)

    grad_val = csend[...].reshape(512, 128)
    ta[:, :, :, 0:128] = nn(nint[:, c].reshape(256, 512), grad_val).reshape(4, 4, 16, 128)
    other = nn(nint[:, 1 - c].reshape(256, 512), grad_val).astype(BF16)
    tcs[:, :, :, 0:128] = other.reshape(4, 4, 16, 128)
    re = pl.ds(pl.multiple_of(half * 512, 512), 512)
    im = pl.ds(pl.multiple_of(half * 512 + SLOT, 512), 512)
    vr, vi, gr, gi = spec_v[re, :], spec_v[im, :], spec_g[re, :], spec_g[im, :]
    tap_grad = tn((vr * gr + vi * gi).astype(BF16), rep[re, :])
    tap_grad = (tap_grad + tn((vr * gi - vi * gr).astype(BF16), rep[im, :])) * (1.0 / SLOT)
    column = lax.broadcasted_iota(jnp.int32, (128, 256), 1)
    sums = tn(skip_grad, jnp.where(column == TAPS + 2, 1.0, 0.0).astype(BF16))
    for k in range(4):
        block = sums[128 * k : 128 * k + 128] + tap_grad * jnp.where(group == k, 1.0, 0.0)
        block = block.reshape(2, 4, 16, 256)
        ta[k, :, :, 128:384] = jnp.where(c == 0, block[0], block[1])
        tcs[k, :, :, 128:384] = jnp.where(c == 0, block[1], block[0]).astype(BF16)
    rs_t = [push(tcs, tcr, sibling)]
    arrived(rs_t)
    for k in range(4):
        total = ta[k] + tcr[k].astype(F32)
        ta[k] = total
        ts2[k] = total.astype(BF16)
    rs_t = ring(x, x_at, lambda to: ts2.at[to], lambda i: tr2.at[i - 1])

    mlp_out = jnp.zeros((128, 512), F32)
    for f in range(4):
        mlp_out = mlp_out + nn(act[:, 512 * f : 512 * f + 512], wd[f].reshape(512, 512))
    outv[...] = hid[...] + mask * mlp_out
    stores = [pltpu.make_async_copy(outv, out_hbm, local_sem.at[5])]
    stores[0].start()

    rs_x1 = reduce_next_x(X1, rs_x1)
    arrived(rs_zd)
    total = accd[:, :, z, :, 0:384]
    for k in range(3):
        total = total + r2a[k].astype(F32)
    acc2a[...] = total
    s3a[...] = total.astype(BF16)
    rs_zd = ring(y, y_at, lambda to: s3a.at[:, to], lambda i: r3a.at[i - 1])
    arrived(rs_yd)
    total = accd[:, y, :, :, 384:512]
    for k in range(3):
        total = total + r2c[k].astype(F32)
    acc2c[...] = total
    s3c[...] = total.astype(BF16)
    rs_yd = ring(z, z_at, lambda to: s3c.at[:, to], lambda i: r3c.at[i - 1])
    rs_yr = reduce_next_y(YR, rs_yr)
    rs_x2 = reduce_next_x(X2, rs_x2)
    arrived(rs_t)
    total = ta[x]
    for k in range(3):
        total = total + tr2[k].astype(F32)
    tacc[...] = total
    ts3[...] = total.astype(BF16)
    rs_t = ring(y, y_at, lambda to: ts3.at[to], lambda i: tr3.at[i - 1])

    taken_back(got_gc)
    grad_val = whole(gcin).astype(BF16)
    weighted = gain_one * (nt(grad_val, weight(VAL, 512)) + nt(ggate[...], weight(GAT, 512)))
    mean_one = jnp.mean(weighted, axis=1, keepdims=True)
    mean_two = jnp.mean(weighted * xh1[...], axis=1, keepdims=True)
    ginv[...] = ghid[...] + (weighted - mean_one - xh1[...] * mean_two) * inv1[...]
    stores.append(pltpu.make_async_copy(ginv, gin_hbm, local_sem.at[6]))
    stores[1].start()

    arrived(rs_zd)
    arrived(rs_yd)
    total = acc2a[:, y]
    for k in range(3):
        total = total + r3a[k].astype(F32)
    acc3d[:, :, 0:384] = total
    s4d[:, :, 0:384] = total.astype(BF16)
    total = acc2c[:, z]
    for k in range(3):
        total = total + r3c[k].astype(F32)
    acc3d[:, :, 384:512] = total
    s4d[:, :, 384:512] = total.astype(BF16)
    rs_d = ring(x, x_at, lambda to: s4d.at[to], lambda i: r4d.at[i - 1])
    reduce_last(X1, rs_x1, y)
    reduce_last(YR, rs_yr, x)
    reduce_last(X2, rs_x2, y)
    s4r[...] = swapped([tail[:, UPA + 768 * q : UPA + 768 * (q + 1)] for q in range(4)])
    rs_z = ring(z, z_at, lambda to: s4r.at[to], lambda i: r4r.at[i - 1])
    arrived(rs_t)
    own, far = tacc[y], tr3[1].astype(F32)
    near = tr3[0].astype(F32) + tr3[2].astype(F32)
    even = y % 2 == 0
    same_group, other_group = own[:, 0:128] + far[:, 0:128], near[:, 0:128]
    extras = own[:, 128:384] + far[:, 128:384] + near[:, 128:384]
    s4e[...] = swapped(
        [
            jnp.where(even, same_group, other_group),
            jnp.where(even, other_group, same_group),
            extras[:, 0:128],
            extras[:, 128:256],
        ]
    )
    rs_t = ring(z, z_at, lambda to: s4e.at[to], lambda i: r4e.at[i - 1])
    arrived(rs_d)
    total = acc3d[x]
    for k in range(3):
        total = total + r4d[k].astype(F32)
    gdown_ref[...] = total
    arrived(rs_z)
    total = s4r[z].astype(F32)
    for k in range(3):
        total = total + r4r[k].astype(F32)
    grest_ref[...] = total
    arrived(rs_t)
    value_low, value_high, extras = jnp.zeros((8, 128), F32), jnp.zeros((8, 128), F32), jnp.zeros((8, 128), F32)
    for k in range(4):
        block = (s4e[z] if k == 0 else r4e[k - 1]).astype(F32)
        is_low = jnp.where(turn(z, 4 - k) < 2, 1.0, 0.0)
        value_low = value_low + block[0:8] * is_low
        value_high = value_high + block[0:8] * (1.0 - is_low)
        extras = extras + block[8:16]
    gearly_ref[0:8] = value_low
    gearly_ref[8:16] = value_high
    gearly_ref[16:24] = extras

    for store in stores:
        store.wait()
    for copy in started:
        if copy is not None:
            copy.wait_send()
    sent_back(sent_c)
    sent_back(sent_n)
    sent_back(sent_g)


def scratch():
    def f32(*shape):
        return pltpu.VMEM(shape, F32)

    def b16(*shape):
        return pltpu.VMEM(shape, BF16)

    copies = 192
    return [
        f32(128, 512), f32(128, 512), f32(128, 512), f32(128, 512),
        b16(1, 4), b16(1, 4), b16(1, 4), b16(4, 1024), b16(NSUB, 4, SUBTAPS), b16(4, 512), b16(4, 2048), b16(16, 512),
        b16(4, 16, 256), b16(4, 16, 768), b16(4, 2, 4, 16, WIDE), b16(4, 2, 4, 4, 16, 512),
        b16(2 * SLOT, SLOT), b16(512, 2 * SLOT), b16(2 * SLOT, 256),
        f32(128, 512), f32(128, 1), b16(128, 512), f32(128, 512), f32(128, 512), f32(128, 512), f32(128, 512),
        b16(128, 512), f32(128, 512), f32(128, 512), b16(128, 512),
        b16(128, 512), f32(128, FF), b16(128, FF), b16(128, FF), f32(128, 512), b16(128, 512), b16(128, 512),
        b16(8, 64, 128), b16(16, 64, 128), b16(8, 64, 128), b16(8, 64, 128),
        b16(8, 64, 128), b16(16, 64, 128), b16(8, 64, 128), b16(8, 64, 128), b16(2, 64, 512), b16(8, 64, 512),
        f32(2 * SLOT, 128), f32(2 * SLOT, 128), f32(2 * SLOT, 128), b16(2 * SLOT, 128),
        b16(4, 2, 64, 128), b16(4, 2, 64, 128), b16(4, 2, 64, 128), b16(4, 2, 256, 128), b16(4, 2, 64, 512),
        f32(4, 4, 16, WIDE), b16(4, 4, 16, WIDE), b16(4, 4, 16, WIDE), b16(4, 4, 16, WIDE), b16(3, 4, 16, WIDE),
        f32(4, 16, WIDE), b16(4, 16, WIDE), b16(3, 16, WIDE), f32(16, WIDE),
        f32(4, 4, 4, 16, 512), b16(4, 4, 4, 16, 512), b16(4, 4, 4, 16, 512), b16(4, 4, 4, 16, 512),
        b16(3, 4, 4, 16, 384), b16(3, 4, 4, 16, 128),
        f32(4, 4, 16, 384), b16(4, 4, 16, 384), b16(3, 4, 16, 384),
        f32(4, 4, 16, 128), b16(4, 4, 16, 128), b16(3, 4, 16, 128),
        f32(4, 16, 512), b16(4, 16, 512), b16(3, 16, 512),
        f32(4, 4, 16, 384), b16(4, 4, 16, 384), b16(4, 4, 16, 384), b16(4, 4, 16, 384), b16(3, 4, 16, 384),
        f32(4, 16, 384), b16(4, 16, 384), b16(3, 16, 384),
        b16(4, 16, 128), b16(3, 16, 128), b16(4, 16, 768), b16(3, 16, 768),
        pltpu.SemaphoreType.DMA((copies,)), pltpu.SemaphoreType.DMA((copies,)), pltpu.SemaphoreType.DMA((16,)),
    ]


def finish(
    out_raw, gin_raw, early_ref, rest_ref, down_raw, sub_ref, w_in_ref, w_up_ref, gain_one_ref, gain_two_ref,
    out_ref, gin_ref, one_ref, in_ref, gsub_ref, skip_ref, mix_ref, two_ref, up_ref, down_ref,
):
    out_ref[...] = out_raw[...]
    gin_ref[...] = gin_raw[...]
    for block, row in enumerate((0, 8, 4, 12)):
        in_ref[:, 128 * block : 128 * (block + 1)] = early_ref[row : row + 4]
    in_ref[:, 512:1024] = rest_ref[4:8, 256:768]
    up_ref[:, 0:768] = rest_ref[0:4]
    up_ref[:, 768:1024] = rest_ref[4:8, 0:256]
    up_ref[:, 1024:1280] = rest_ref[8:12, 512:768]
    up_ref[:, 1280:2048] = rest_ref[12:16]
    mix_ref[...] = rest_ref[8:12, 0:512]
    down_ref[...] = down_raw[...]
    extras = jnp.concatenate([early_ref[16:20], early_ref[20:24]], axis=1)
    diagonal = lax.broadcasted_iota(jnp.int32, (4, 4), 0) == lax.broadcasted_iota(jnp.int32, (4, 4), 1)
    lane = lax.broadcasted_iota(jnp.int32, (4, 256), 1)

    def as_row(column):
        return jnp.sum(jnp.where(diagonal, column, 0.0), axis=0, keepdims=True)

    skip_ref[...] = as_row(jnp.sum(jnp.where(lane == TAPS + 2, extras, 0.0), axis=1, keepdims=True))
    for ref, gain, weight, grad in (
        (one_ref, gain_one_ref, w_in_ref, in_ref),
        (two_ref, gain_two_ref, w_up_ref, up_ref),
    ):
        along = jnp.sum(weight[...].astype(F32) * grad[...], axis=1, keepdims=True)
        ref[...] = as_row(along) / gain[...].astype(F32)
    taps = [sub_ref[i].astype(F32) for i in range(NSUB)]
    grads = [extras[:, SUBTAPS * i : SUBTAPS * (i + 1)] for i in range(NSUB)]
    squares, along = jnp.zeros((4, SUBTAPS), F32), jnp.zeros((4, SUBTAPS), F32)
    for i in range(NSUB):
        squares = squares + taps[i] * taps[i] * 0.5**i
        along = along + taps[i] * grads[i]
    norm = lax.rsqrt(jnp.sum(squares, axis=1, keepdims=True) + EPSILON)
    pull = norm * norm * norm * jnp.sum(along, axis=1, keepdims=True)
    for i in range(NSUB):
        gsub_ref[i] = norm * grads[i] - 0.5**i * taps[i] * pull


def body(
    inputs,
    cotangent,
    lengths,
    gain_first,
    proj_in,
    sub_kernels,
    skip_gain,
    proj_out,
    gain_second,
    mlp_up,
    mlp_down,
):
    forward, inverse, repeat = transforms()
    taps = sub_kernels.transpose(0, 2, 1)
    vmem = pl.BlockSpec(memory_space=pltpu.VMEM)
    smem = pl.BlockSpec(memory_space=pltpu.SMEM)
    anywhere = pl.BlockSpec(memory_space=pl.ANY)

    def f32(*shape):
        return jax.ShapeDtypeStruct(shape, F32)

    outputs, grad_inputs, early, rest, down = pl.pallas_call(
        fused,
        out_shape=(f32(128, 512), f32(128, 512), f32(24, 128), f32(16, 768), f32(16, 512)),
        in_specs=[anywhere, anywhere, smem] + [anywhere] * 11,
        out_specs=(anywhere, anywhere, vmem, vmem, vmem),
        scratch_shapes=scratch(),
        compiler_params=pltpu.CompilerParams(
            collective_id=0, has_side_effects=True, vmem_limit_bytes=60 * 2**20
        ),
        name="block",
    )(
        inputs.reshape(128, 512),
        cotangent.reshape(128, 512),
        lengths,
        gain_first.reshape(1, 4),
        gain_second.reshape(1, 4),
        skip_gain.reshape(1, 4),
        proj_in,
        taps,
        proj_out,
        mlp_up,
        mlp_down,
        jnp.asarray(forward),
        jnp.asarray(inverse),
        jnp.asarray(repeat),
    )
    outputs, grad_inputs, one, w_in, g_sub, skip, w_out, two, up, down = pl.pallas_call(
        finish,
        out_shape=(
            f32(128, 512), f32(128, 512), f32(1, 4), f32(4, 1024), f32(NSUB, 4, SUBTAPS), f32(1, 4),
            f32(4, 512), f32(1, 4), f32(4, 2048), f32(16, 512),
        ),
        in_specs=[vmem] * 10,
        out_specs=(vmem,) * 10,
        name="finish",
    )(
        outputs, grad_inputs, early, rest, down, taps, proj_in, mlp_up,
        gain_first.reshape(1, 4), gain_second.reshape(1, 4),
    )
    return (
        outputs.reshape(2, 64, 512),
        grad_inputs.reshape(2, 64, 512),
        one.reshape(4),
        w_in,
        g_sub.transpose(0, 2, 1),
        skip.reshape(4),
        w_out,
        two.reshape(4),
        up,
        down,
    )


def solution(mesh):
    in_specs = (
        P("dp", "seq", None),
        P("dp", "seq", None),
        P("dp"),
        P(("dp", "seq")),
        P(("dp", "seq"), None),
        P(None, None, ("dp", "seq")),
        P(("dp", "seq")),
        P(("dp", "seq"), None),
        P(("dp", "seq")),
        P(("dp", "seq"), None),
        P(("dp", "seq"), None),
    )
    out_specs = (
        P("dp", "seq", None),
        P("dp", "seq", None),
        P(("dp", "seq")),
        P(("dp", "seq"), None),
        P(None, None, ("dp", "seq")),
        P(("dp", "seq")),
        P(("dp", "seq"), None),
        P(("dp", "seq")),
        P(("dp", "seq"), None),
        P(("dp", "seq"), None),
    )
    return jax.shard_map(body, mesh=mesh, in_specs=in_specs, out_specs=out_specs, check_vma=False)
```

time: 106 us -> 79.1 us (0.75)
  local copies, waits for them, and re-layouts: 13.5 us -> 0 us
  Pallas kernels: 90 us -> 78 us
  other arithmetic: 1.47 us -> 0 us
    pallas_call x1 -> x2, Pallas kernels: 90 us -> 78 us  [the longest x1 75.8 us: body(): pl.pallas_call(fused, out_shape=(f32(128, 512), f32(128, 512), f32(24, 12...]
    unnamed x7 -> x0, local copies, waits for them, and re-layouts: 6.02 us -> none
    slice x5 -> x0, local copies, waits for them, and re-layouts: 2.78 us -> none  [the longest x1 0.74 us: body(): rows[:, EXT + TAPS + 1]]
    broadcast_in_dim x5 -> x0, local copies, waits for them, and re-layouts: 2.27 us -> none  [the longest x1 0.76 us: body(): gain_first[:, None]]
    reshape x4 -> x0, local copies, waits for them, and re-layouts: 1.66 us -> none  [the longest x1 0.86 us: body(): rows = gpack.reshape(4, 4, 1024).transpose(1, 0, 2).reshape(4, WIDE)]
    concatenate x2 -> x0, other arithmetic: 1.23 us -> none  [the longest x1 0.62 us: body(): jnp.concatenate([rows[:, UPA:GAT], rows[:, UPB:END]], axis=1)]
where the time goes in v2:
time: 79.1 us; the launch traced here: 78.6 us
  Pallas kernels  78 us (99%)
    pallas_call x1, Pallas kernels, body(): pl.pallas_call(fused, out_shape=(f32(128, 512), f32(128, 512), f32(24, 12...  75.8 us
    pallas_call x1, Pallas kernels, body(): pl.pallas_call(finish, out_shape=(f32(128, 512), f32(128, 512), f32(1, 4)...  2.16 us

profile of v2, /device:TPU:0, one launch (start us, length us, event | category | flops | bytes accessed | tf_op | source)
XLA Modules:
  0.0 78.6 jit_solution(13229940324616144853)
XLA Ops:
  0.6 75.8 %block.1 = (f32[128,512]{1,0:T(8,128)}, f32[128,512]{1,0:T(8,128)}, f32[24,128]{1,0:T(8,128)}, f32[16,768]{1,0:T(8,128)}, f32[16,512]{1,0:T(8,128)}) custom-call(f32[128,512]{1,0:T(8,128)} %bitcast.12, f32[128,512]{1,0:T(8,128)} %bitcast.13, s32[2]{0:T(128)} %len_ref.1, bf16[1,4]{1,0:T(2,128)(2,1)} %bitcast.16, bf16[1,4]{1,0:T(2,128)(2,1)} %bitcast.18, ...), custom_call_target="tpu_custom_call" | custom-call | tf_op jit(solution)/shard_map/block/pallas_call | solution.py:782
  76.5 2.2 %finish.1 = (f32[128,512]{1,0:T(8,128)}, f32[128,512]{1,0:T(8,128)}, f32[1,4]{1,0:T(1,128)}, f32[4,1024]{1,0:T(4,128)}, f32[5,4,32]{2,1,0:T(4,128)}, /*index=5*/...) custom-call(f32[128,512]{1,0:T(8,128)} %get-tuple-element.25.out_raw, ...), custom_call_target="tpu_custom_call" | custom-call | tf_op jit(solution)/shard_map/finish/pallas_call | solution.py:808
